TPU v7x, 512 devices: a whole 4x4x16 slice. The times are simulated.
512 devices in a mesh: bins: 128 (over z_lo, y, x), ch: 4 (over z_hi, core).
Axes of the slice: x: 4, y: 4, z: 16 (z_hi: 2, z_lo: 8; z = z_hi * 8 + z_lo), core: 2. Of those that a mesh axis runs over, the one named last changes fastest.
Arguments:
- inputs: bfloat16 [65536, 768], P('bins', 'ch'), may hold values from -6 to 6
- cotangent: bfloat16 [65536, 768], P('bins', 'ch'), may hold values from -6 to 6
- first_kernel_weight: bfloat16 [3, 768, 768], P(None, 'ch'), may hold values from -0.125 to 0.125
- second_kernel_weight: bfloat16 [3, 768, 768], P(None, 'ch'), may hold values from -0.125 to 0.125
Outputs:
- activations: bfloat16 [65536, 768], P('bins', 'ch')
- input_grad: bfloat16 [65536, 768], P('bins', 'ch')
- grad_near: bfloat16 [3, 768, 768], P(None, 'ch')
- grad_far: bfloat16 [3, 768, 768], P(None, 'ch')
All inputs are finite; a program needn't handle non-finite values.
Results may differ from a plain program's by a relative error of at most 0.013.
Values may be sent and summed in bfloat16 or wider, within the bound.
A program may use at most 64 MiB of HBM per device.

v0:
```python
import math

import jax
import jax.numpy as jnp
from jax import lax
from jax.sharding import PartitionSpec as P

DILATION_FIRST = 512
DILATION_SECOND = 2048


gelu_coeff = 0.7978845608


def passed_along(block, axis, distance):
    devices = range(lax.axis_size(axis))
    route = [(i - distance, i) for i in devices if i - distance in devices]
    return lax.ppermute(block, axis, route)


def gelu_value(values):
    inner = gelu_coeff * (values + 0.044715 * values * values * values)
    return 0.5 * values * (1.0 + jnp.tanh(inner))


def gelu_slope(values):
    inner = gelu_coeff * (values + 0.044715 * values * values * values)
    tangent = jnp.tanh(inner)
    return 0.5 * (1.0 + tangent) + 0.5 * values * (1.0 - tangent * tangent) * gelu_coeff * (
        1.0 + 3.0 * 0.044715 * values * values
    )


def against_kernel(full_grad, kernel):
    return lax.dot_general(
        full_grad, kernel, (((1,), (1,)), ((), ())), preferred_element_type=jnp.float32
    )


def over_rows(left_rows, right_rows):
    return lax.dot_general(
        left_rows, right_rows, (((0,), (0,)), ((), ())), preferred_element_type=jnp.float32
    )


def device_hops(dilation, bin_rows):
    return max(dilation // bin_rows, 1)


def body(inputs, cotangent, first_kernel_weight, second_kernel_weight):
    bin_rows = inputs.shape[0]
    residual_blocks = (
        (first_kernel_weight, DILATION_FIRST),
        (second_kernel_weight, DILATION_SECOND),
    )
    current = inputs
    stored = []
    for weight, dilation in residual_blocks:
        hop_count = device_hops(dilation, bin_rows)
        activated = gelu_value(current.astype(jnp.float32)).astype(jnp.bfloat16)
        got_earlier = passed_along(activated, "bins", hop_count)
        got_later = passed_along(activated, "bins", -hop_count)
        tap_rows = (got_earlier, activated, got_later)
        partial_value = jnp.dot(got_earlier, weight[0], preferred_element_type=jnp.float32)
        partial_value = partial_value + jnp.dot(
            activated, weight[1], preferred_element_type=jnp.float32
        )
        partial_value = partial_value + jnp.dot(
            got_later, weight[2], preferred_element_type=jnp.float32
        )
        conv_out = lax.psum_scatter(partial_value, "ch", scatter_dimension=1, tiled=True)
        stored.append((current, tap_rows))
        current = (current.astype(jnp.float32) + conv_out).astype(jnp.bfloat16)
    norm_scale = 1.0 / math.sqrt(bin_rows * lax.axis_size("bins"))
    gradient = cotangent
    local_grads = [None, None]
    kernel_grads = [None, None]
    for block_number in (1, 0):
        weight, dilation = residual_blocks[block_number]
        hop_count = device_hops(dilation, bin_rows)
        previous, tap_rows = stored[block_number]
        full_grad = lax.all_gather(gradient, "ch", axis=1, tiled=True)
        got_later = passed_along(full_grad, "bins", -hop_count)
        got_earlier = passed_along(full_grad, "bins", hop_count)
        back_sum = against_kernel(got_later, weight[0])
        back_sum = back_sum + against_kernel(full_grad, weight[1])
        back_sum = back_sum + against_kernel(got_earlier, weight[2])
        local_kernel = jnp.stack(
            [
                over_rows(tap_rows[0], full_grad),
                over_rows(tap_rows[1], full_grad),
                over_rows(tap_rows[2], full_grad),
            ]
        )
        local_grads[block_number] = local_kernel
        gradient = (
            gradient.astype(jnp.float32) + gelu_slope(previous.astype(jnp.float32)) * back_sum
        ).astype(jnp.bfloat16)
    summed_near, summed_far = lax.psum((local_grads[0], local_grads[1]), "bins")
    kernel_grads[0] = (summed_near * norm_scale).astype(jnp.bfloat16)
    kernel_grads[1] = (summed_far * norm_scale).astype(jnp.bfloat16)
    return (current, gradient, kernel_grads[0], kernel_grads[1])


def solution(mesh):
    return jax.shard_map(
        body,
        mesh=mesh,
        in_specs=(P("bins", "ch"), P("bins", "ch"), P(None, "ch", None), P(None, "ch", None)),
        out_specs=(P("bins", "ch"), P("bins", "ch"), P(None, "ch", None), P(None, "ch", None)),
        check_vma=False,
    )
```

profile of v0, /device:TPU:6, one launch (start us, length us, event | category | flops | bytes accessed | tf_op | source)
XLA Modules:
  0.0 2218.4 jit_solution(16712324065106982721)
XLA Ops:
  8.4 3.4 collective-permute-start
  11.8 2.4 collective-permute-start.1
  14.2 1.6 fusion.49
  17.3 4.8 collective-permute-done.1
  22.1 1.6 add_add_fusion.1
  23.8 89.0 %reduce-scatter.3.cloned.1.call-done = f32[512,192]{0,1:T(8,128)} async-done(((f32[512,768]{0,1:T(8,128)}), f32[512,192]{0,1:T(8,128)}) %reduce-scatter.3.cloned.1.call-update) | async-done | bytes 393232 | tf_op jit(solution)/shard_map/reduce_scatter | solution.py:71
  113.9 3.4 collective-permute-start.2
  119.1 2.4 collective-permute-done.2
  122.0 3.7 collective-permute-done.3
  125.7 1.6 add_add_fusion
  128.2 25.1 %all_gather.6 = bf16[512,768]{0,1:T(8,128)(2,1)S(1)} all-gather(bf16[512,192]{0,1:T(8,128)(2,1)S(1)} %copy-done.3), channel_id=1, replica_groups=mesh['bins'=128,'ch'=4] {'ch'}, dimensions={1}, use_global_device_ids=true | all-gather | bytes 983040 | tf_op jit(solution)/shard_map/all_gather | solution.py:82
  153.3 2.2 collective-permute-start.5
  157.1 15.6 collective-permute-done.5
  173.1 4.9 collective-permute-done.4
  178.4 29.5 %all_gather.7 = bf16[512,768]{0,1:T(8,128)(2,1)S(1)} all-gather(bf16[512,192]{0,1:T(8,128)(2,1)S(1)} %fusion.6), channel_id=1, replica_groups=mesh['bins'=128,'ch'=4] {'ch'}, dimensions={1}, use_global_device_ids=true | all-gather | bytes 983040 | tf_op jit(solution)/shard_map/all_gather | solution.py:82
  209.2 1.3 pad_maximum_fusion
  211.8 1.4 pad_maximum_fusion.1
  213.2 16.0 collective-permute-start.7
  229.2 1.9 collective-permute-start.6
  231.5 15.0 collective-permute-done.7
  246.8 5.9 collective-permute-done.6
  253.9 1.7 fusion.26
  255.7 1952.7 %all-reduce.3.cloned.1.call-done = (f32[3,192,768]{2,1,0:T(8,128)}, f32[3,192,768]{2,1,0:T(8,128)}) async-done(((f32[3,192,768]{2,1,0:T(8,128)}, f32[3,192,768]{2,1,0:T(8,128)}), (f32[3,192,768]{2,1,0:T(8,128)}, f32[3,192,768]{2,1,0:T(8,128)})) %all-reduce.3.cloned.1.call-update) | async-done | bytes 3538960 | tf_op jit(solution)/shard_map/psum | solution.py:99
  2208.3 3.5 multiply_convert_fusion
  (35 shorter events, 13.9 us)
Async XLA Ops:
  7.2 9.7 copy-start.1
  7.2 105.6 %reduce-scatter.3.cloned.1.call-start = ((), (), s32[]{:S(2)}) async-start(), calls=%async_computation.2 | async-start | bytes 1966080 | tf_op jit(solution)/shard_map/reduce_scatter | solution.py:71
  8.4 8.5 collective-permute-start
  11.8 10.4 collective-permute-start.1
  23.7 89.0 %copy-start.2 = (bf16[512,192]{0,1:T(8,128)(2,1)S(1)}, bf16[512,192]{0,1:T(8,128)(2,1)}, u32[]{:S(2)}) copy-start(bf16[512,192]{0,1:T(8,128)(2,1)} %param.4) | copy-start | bytes 589828
  23.7 94.9 %copy-start = (bf16[3,192,768]{2,1,0:T(8,128)(2,1)S(1)}, bf16[3,192,768]{2,1,0:T(8,128)(2,1)}, u32[]{:S(2)}) copy-start(bf16[3,192,768]{2,1,0:T(8,128)(2,1)} %param.7) | copy-start | bytes 2654212
  23.8 230.2 %reduce-scatter.5.cloned.1.call-start = ((), (), s32[]{:S(2)}) async-start(), calls=%async_computation.3 | async-start | bytes 1966080 | tf_op jit(solution)/shard_map/reduce_scatter | solution.py:71
  113.9 7.6 collective-permute-start.2
  117.3 8.3 collective-permute-start.3
  127.3 0.9 copy-start.3
  127.3 2081.0 %all-reduce.3.cloned.1.call-start = ((), (), s32[]{:S(2)}) async-start(), calls=%async_computation.4 | async-start | bytes 7077888 | tf_op jit(solution)/shard_map/psum | solution.py:99
  153.3 19.4 collective-permute-start.5
  155.5 22.4 %collective-permute-start.4 = (bf16[512,768]{0,1:T(8,128)(2,1)S(1)}, bf16[512,768]{0,1:T(8,128)(2,1)S(1)}, u32[]{:S(2)}, u32[]{:S(2)}) collective-permute-start(bf16[512,768]{0,1:T(8,128)(2,1)S(1)} %all_gather.6), channel_id=1, source_target_pairs={{16,0},{20,4},{24,8},{28,12},{32,16},{36,20},{40,24},{44,28},{48,3... | collective-permute-start | bytes 2359304 | tf_op jit(solution)/shard_map/ppermute | solution.py:18
  213.2 33.3 %collective-permute-start.7 = (bf16[512,768]{0,1:T(8,128)(2,1)S(1)}, bf16[512,768]{0,1:T(8,128)(2,1)S(1)}, u32[]{:S(2)}, u32[]{:S(2)}) collective-permute-start(bf16[512,768]{0,1:T(8,128)(2,1)S(1)} %all_gather.7), channel_id=1, source_target_pairs={{0,4},{4,8},{8,12},{12,16},{16,20},{20,24},{24,28},{28,32},{32,36}... | collective-permute-start | bytes 2359304 | tf_op jit(solution)/shard_map/ppermute | solution.py:18
  229.2 23.5 %collective-permute-start.6 = (bf16[512,768]{0,1:T(8,128)(2,1)S(1)}, bf16[512,768]{0,1:T(8,128)(2,1)S(1)}, u32[]{:S(2)}, u32[]{:S(2)}) collective-permute-start(bf16[512,768]{0,1:T(8,128)(2,1)S(1)} %all_gather.7), channel_id=1, source_target_pairs={{4,0},{8,4},{12,8},{16,12},{20,16},{24,20},{28,24},{32,28},{36,32}... | collective-permute-start | bytes 2359304 | tf_op jit(solution)/shard_map/ppermute | solution.py:18
Sparse Core Ops, SparseCore 0:
  23.9 88.8 reduce-scatter.2
  127.5 77.1 reduce-scatter.4
  213.3 1994.9 all-reduce.2
where the time goes:
time: 2220 us
  waiting for transfers between devices  2100 us (95%)
  blocking collectives  54.5 us (2%)
  starting transfers between devices  32 us (1%)
    psum x1, waiting for transfers between devices, body(): summed_near, summed_far = lax.psum((local_grads[0], local_grads[1]), 'bins')  1950 us
    reduce_scatter x2, waiting for transfers between devices, body(): lax.psum_scatter(partial_value, 'ch', scatter_dimension=1, tiled=True)  89 us
    all_gather x2, blocking collectives, body(): full_grad = lax.all_gather(gradient, 'ch', axis=1, tiled=True)  54.5 us
    ppermute x8, waiting for transfers between devices, passed_along(): return lax.ppermute(block, axis, route)  53.5 us
  transfers between devices with their start and end apart: 11, of which 10 were waited for; matrix products, arithmetic and copies ran while one was open for 1% of the time, Pallas kernels for 0%

commit v1 on v0

--- a/solution.py
+++ b/solution.py
@@ -3,10 +3,15 @@
 import jax
 import jax.numpy as jnp
 from jax import lax
+from jax.experimental import pallas as pl
+from jax.experimental.pallas import tpu as pltpu
 from jax.sharding import PartitionSpec as P
 
 DILATION_FIRST = 512
 DILATION_SECOND = 2048
+MESH = pl.DeviceIdType.MESH
+NUM_X, NUM_Y, NUM_Z = 4, 4, 8
+UNITS = 27
 
 
 gelu_coeff = 0.7978845608
@@ -45,6 +50,180 @@
 
 def device_hops(dilation, bin_rows):
     return max(dilation // bin_rows, 1)
+
+
+class Place:
+    def __init__(self):
+        b = lax.axis_index("bins")
+        self.b = b
+        self.ch = lax.axis_index("ch")
+        self.x = lax.rem(b, 4)
+        self.y = lax.rem(lax.div(b, 4), 4)
+        self.z = lax.div(b, 16)
+
+    def shifted(self, axis, d):
+        x, y, z = self.x, self.y, self.z
+        if axis == "x":
+            x = lax.rem(x + d, 4)
+        elif axis == "y":
+            y = lax.rem(y + d, 4)
+        else:
+            z = lax.rem(z + d, 8)
+        return (z * 16 + y * 4 + x, self.ch)
+
+    def coordinate(self, axis):
+        return {"x": self.x, "y": self.y, "z": self.z}[axis]
+
+
+AXES = (("x", "y"), ("y", "x"))
+
+
+def unit_place(linear):
+    tap, rest = divmod(linear, 72)
+    row, col = divmod(rest, 6)
+    return tap, row * 16, col * 128
+
+
+def send(src, dst, send_sem, recv_sem, target):
+    copy = pltpu.make_async_remote_copy(
+        src_ref=src,
+        dst_ref=dst,
+        send_sem=send_sem,
+        recv_sem=recv_sem,
+        device_id=target,
+        device_id_type=MESH,
+    )
+    copy.start()
+    return copy
+
+
+def sum_kernel(near_ref, far_ref, near_out, far_out, d1, r1, d2, r2, d3, r3, g3, g2, g1,
+               s1, q1, s2, q2, s3, q3, s4, q4, s5, q5, s6, q6):
+    me = Place()
+    barrier = pltpu.get_barrier_semaphore()
+    for axis, n in (("x", 4), ("y", 4), ("z", 8)):
+        for d in range(1, n):
+            pl.semaphore_signal(barrier, inc=1, device_id=me.shifted(axis, d), device_id_type=MESH)
+    sent = []
+    parts = [(b, p) for b in (1, 0) for p in (0, 1)]
+    sources = (near_ref, far_ref)
+    results = (near_out, far_out)
+    for b, p in parts:
+        for q in range(4):
+            for r in range(UNITS):
+                tap, row, col = unit_place(p * 108 + q * UNITS + r)
+                d1[2 * b + p, q, r] = sources[b][tap, row : row + 16, col : col + 128].astype(jnp.bfloat16)
+    pl.semaphore_wait(barrier, 13)
+
+    first = {}
+    for b, p in parts:
+        i = 2 * b + p
+        axis = AXES[p][0]
+        here = me.coordinate(axis)
+        for d in (1, 2, 3):
+            first[i, d] = send(d1.at[i, lax.rem(here + d, 4)], r1.at[i, d - 1], s1.at[i, d - 1], q1.at[i, d - 1],
+                               me.shifted(axis, d))
+    second = {}
+    for b, p in parts:
+        i = 2 * b + p
+        here = me.coordinate(AXES[p][0])
+        for d in (1, 2, 3):
+            first[i, d].wait_recv()
+        for r in range(0, UNITS, 9):
+            total = d1[i, here, r : r + 9].astype(jnp.float32)
+            for d in range(3):
+                total = total + r1[i, d, r : r + 9].astype(jnp.float32)
+            d2[i, r : r + 9] = total.astype(jnp.bfloat16)
+        d2[i, UNITS:] = jnp.zeros((32 - UNITS, 16, 128), jnp.bfloat16)
+        axis = AXES[p][1]
+        there = me.coordinate(axis)
+        for d in (1, 2, 3):
+            second[i, d] = send(d2.at[i, pl.ds(lax.rem(there + d, 4) * 8, 8)], r2.at[i, d - 1], s2.at[i, d - 1],
+                                q2.at[i, d - 1], me.shifted(axis, d))
+    third = {}
+    for b, p in parts:
+        i = 2 * b + p
+        there = me.coordinate(AXES[p][1])
+        for d in (1, 2, 3):
+            second[i, d].wait_recv()
+        total = d2[i, pl.ds(there * 8, 8)].astype(jnp.float32)
+        for d in range(3):
+            total = total + r2[i, d].astype(jnp.float32)
+        d3[i] = total.astype(jnp.bfloat16)
+        for d in range(1, 8):
+            third[i, d] = send(d3.at[i, lax.rem(me.z + d, 8)], r3.at[i, d - 1], s3.at[i, d - 1], q3.at[i, d - 1],
+                               me.shifted("z", d))
+    fourth = {}
+    scale = 1.0 / math.sqrt(65536)
+    for b, p in parts:
+        i = 2 * b + p
+        for d in range(1, 8):
+            third[i, d].wait_recv()
+        total = d3[i, me.z].astype(jnp.float32)
+        for d in range(7):
+            total = total + r3[i, d].astype(jnp.float32)
+        g3[i, me.z] = (total * scale).astype(jnp.bfloat16)
+        for d in range(1, 8):
+            fourth[i, d] = send(g3.at[i, me.z], g3.at[i, me.z], s4.at[i, d - 1], q4.at[i, d - 1],
+                                me.shifted("z", d))
+    fifth = {}
+    for b, p in parts:
+        i = 2 * b + p
+        axis = AXES[p][1]
+        there = me.coordinate(axis)
+        for d in range(1, 8):
+            fourth[i, d].wait_recv()
+        for d in (1, 2, 3):
+            fifth[i, d] = send(g3.at[i], g2.at[i, pl.ds(there * 8, 8)], s5.at[i, d - 1], q5.at[i, d - 1],
+                               me.shifted(axis, d))
+        g2[i, pl.ds(there * 8, 8)] = g3[i]
+    sixth = {}
+    for b, p in parts:
+        i = 2 * b + p
+        axis = AXES[p][0]
+        here = me.coordinate(axis)
+        for d in (1, 2, 3):
+            fifth[i, d].wait_recv()
+        for d in (1, 2, 3):
+            sixth[i, d] = send(g2.at[i, pl.ds(0, UNITS)], g1.at[i, here], s6.at[i, d - 1], q6.at[i, d - 1],
+                               me.shifted(axis, d))
+        g1[i, here] = g2[i, :UNITS]
+    for b, p in parts:
+        i = 2 * b + p
+        for d in (1, 2, 3):
+            sixth[i, d].wait_recv()
+        for q in range(4):
+            for r in range(UNITS):
+                tap, row, col = unit_place(p * 108 + q * UNITS + r)
+                results[b][tap, row : row + 16, col : col + 128] = g1[i, q, r]
+    for group in (first, second, third, fourth, fifth, sixth):
+        for copy in group.values():
+            copy.wait_send()
+
+
+def summed(near, far):
+    out = jax.ShapeDtypeStruct((3, 192, 768), jnp.bfloat16)
+    vmem = pl.BlockSpec(memory_space=pltpu.VMEM)
+
+    def buffer(*lead):
+        return pltpu.VMEM((4,) + lead + (16, 128), jnp.bfloat16)
+
+    def sems(n):
+        return [pltpu.SemaphoreType.DMA((4, n))] * 2
+
+    return pl.pallas_call(
+        sum_kernel,
+        out_shape=(out, out),
+        in_specs=[vmem] * 2,
+        out_specs=(vmem, vmem),
+        scratch_shapes=[
+            buffer(4, UNITS), buffer(3, UNITS), buffer(32), buffer(3, 8), buffer(8), buffer(7),
+            buffer(8), buffer(32), buffer(4, UNITS),
+        ] + sems(3) + sems(3) + sems(7) + sems(7) + sems(3) + sems(3),
+        compiler_params=pltpu.CompilerParams(
+            collective_id=0, has_side_effects=True, vmem_limit_bytes=48 * 2**20
+        ),
+    )(near, far)
 
 
 def body(inputs, cotangent, first_kernel_weight, second_kernel_weight):
@@ -71,10 +250,8 @@
         conv_out = lax.psum_scatter(partial_value, "ch", scatter_dimension=1, tiled=True)
         stored.append((current, tap_rows))
         current = (current.astype(jnp.float32) + conv_out).astype(jnp.bfloat16)
-    norm_scale = 1.0 / math.sqrt(bin_rows * lax.axis_size("bins"))
     gradient = cotangent
     local_grads = [None, None]
-    kernel_grads = [None, None]
     for block_number in (1, 0):
         weight, dilation = residual_blocks[block_number]
         hop_count = device_hops(dilation, bin_rows)
@@ -96,10 +273,8 @@
         gradient = (
             gradient.astype(jnp.float32) + gelu_slope(previous.astype(jnp.float32)) * back_sum
         ).astype(jnp.bfloat16)
-    summed_near, summed_far = lax.psum((local_grads[0], local_grads[1]), "bins")
-    kernel_grads[0] = (summed_near * norm_scale).astype(jnp.bfloat16)
-    kernel_grads[1] = (summed_far * norm_scale).astype(jnp.bfloat16)
-    return (current, gradient, kernel_grads[0], kernel_grads[1])
+    grad_near, grad_far = summed(local_grads[0], local_grads[1])
+    return (current, gradient, grad_near, grad_far)
 
 
 def solution(mesh):

time: 2220 us -> 265 us (0.12)
  waiting for transfers between devices: 2100 us -> 72.6 us
  Pallas kernels: 0 us -> 83.3 us
    psum x1 -> x0, waiting for transfers between devices: 1950 us -> none  [body(): summed_near, summed_far = lax.psum((local_grads[0], local_grads[1]), 'bins')]
    pallas_call x0 -> x1, Pallas kernels: none -> 83.3 us  [summed(): pl.pallas_call(sum_kernel, out_shape=(out, out), in_specs=[vmem] * 2, out...]
    ppermute x8, waiting for transfers between devices: 53.5 us -> 11.4 us  [passed_along(): return lax.ppermute(block, axis, route)]
    reduce_scatter x2, waiting for transfers between devices: 89 us -> 61.2 us  [body(): lax.psum_scatter(partial_value, 'ch', scatter_dimension=1, tiled=True)]
  transfers between devices with their start and end apart: 11 -> 10, of which waited for: 10 -> 5; matrix products, arithmetic and copies ran while one was open for 1% -> 5% of each run, Pallas kernels for 0% -> 31%
where the time goes in v1:
time: 265 us
  Pallas kernels  83.3 us (31%)
  waiting for transfers between devices  72.6 us (27%)
  blocking collectives  49.7 us (19%)
  starting transfers between devices  22.7 us (9%)
  between operations  14.3 us (5%)
  matrix products  13.8 us (5%)
  other arithmetic  4.24 us (2%)
  local copies, waits for them, and re-layouts  4.02 us (2%)
    pallas_call x1, Pallas kernels, summed(): pl.pallas_call(sum_kernel, out_shape=(out, out), in_specs=[vmem] * 2, out...  83.3 us
    reduce_scatter x2, waiting for transfers between devices, body(): lax.psum_scatter(partial_value, 'ch', scatter_dimension=1, tiled=True)  61.2 us
    all_gather x2, blocking collectives, body(): full_grad = lax.all_gather(gradient, 'ch', axis=1, tiled=True)  49.7 us
    ppermute x8, starting transfers between devices, passed_along(): return lax.ppermute(block, axis, route)  22.6 us
    ppermute x8, waiting for transfers between devices, passed_along(): return lax.ppermute(block, axis, route)  11.4 us
  transfers between devices with their start and end apart: 10, of which 5 were waited for; matrix products, arithmetic and copies ran while one was open for 5% of the time, Pallas kernels for 31%

profile of v1, /device:TPU:6, one launch (start us, length us, event | category | flops | bytes accessed | tf_op | source)
XLA Modules:
  0.0 264.7 jit_solution(8892396137483560392)
XLA Ops:
  7.2 1.1 fusion.16
  8.4 3.4 %collective-permute-start = (bf16[512,192]{0,1:T(8,128)(2,1)S(1)}, bf16[512,192]{0,1:T(8,128)(2,1)S(1)}, u32[]{:S(2)}, u32[]{:S(2)}) collective-permute-start(bf16[512,192]{0,1:T(8,128)(2,1)S(1)} %fusion.16), channel_id=1, source_target_pairs={{0,4},{4,8},{8,12},{12,16},{16,20},{20,24},{24,28},{28,32},{32,36}... | collective-permute-start | bytes 589832 | tf_op jit(solution)/shard_map/ppermute | solution.py:23
  11.8 2.4 collective-permute-start.1
  14.2 1.6 fusion.49
  17.3 4.8 %collective-permute-done.1 = bf16[512,192]{0,1:T(8,128)(2,1)S(1)} collective-permute-done((bf16[512,192]{0,1:T(8,128)(2,1)S(1)}, bf16[512,192]{0,1:T(8,128)(2,1)S(1)}, u32[]{:S(2)}, u32[]{:S(2)}) %collective-permute-start.1) | collective-permute-done | bytes 196640 | tf_op jit(solution)/shard_map/ppermute | solution.py:23
  22.1 1.6 add_add_fusion.1
  24.7 21.2 %all_gather.6 = bf16[512,768]{0,1:T(8,128)(2,1)S(1)} all-gather(bf16[512,192]{0,1:T(8,128)(2,1)S(1)} %copy-done.7), channel_id=1, replica_groups=mesh['bins'=128,'ch'=4] {'ch'}, dimensions={1}, use_global_device_ids=true | all-gather | bytes 983040 | tf_op jit(solution)/shard_map/all_gather | solution.py:259
  45.9 4.3 %collective-permute-start.5 = (bf16[512,768]{0,1:T(8,128)(2,1)S(1)}, bf16[512,768]{0,1:T(8,128)(2,1)}, u32[]{:S(2)}, u32[]{:S(2)}) collective-permute-start(bf16[512,768]{0,1:T(8,128)(2,1)S(1)} %all_gather.6), channel_id=1, source_target_pairs={{0,16},{4,20},{8,24},{12,28},{16,32},{20,36},{24,40},{28,44},{32,4... | collective-permute-start | bytes 2359304 | tf_op jit(solution)/shard_map/ppermute | solution.py:23
  50.2 1.3 collective-permute-start.4
  51.5 61.2 %reduce-scatter.3.cloned.1.call-done = f32[512,192]{0,1:T(8,128)} async-done(((f32[512,768]{0,1:T(8,128)}), f32[512,192]{0,1:T(8,128)}) %reduce-scatter.3.cloned.1.call-update) | async-done | bytes 393232 | tf_op jit(solution)/shard_map/reduce_scatter | solution.py:250
  112.7 1.2 fusion.12
  113.9 3.4 %collective-permute-start.2 = (bf16[512,192]{0,1:T(8,128)(2,1)S(1)}, bf16[512,192]{0,1:T(8,128)(2,1)S(1)}, u32[]{:S(2)}, u32[]{:S(2)}) collective-permute-start(bf16[512,192]{0,1:T(8,128)(2,1)S(1)} %get-tuple-element.8), channel_id=1, source_target_pairs={{0,16},{4,20},{8,24},{12,28},{16,32},{20,36},{24,40},{28,44},{32,4... | collective-permute-start | bytes 589832 | tf_op jit(solution)/shard_map/ppermute | solution.py:23
  117.3 1.3 collective-permute-start.3
  119.1 2.4 collective-permute-done.2
  122.6 3.0 %collective-permute-done.3 = bf16[512,192]{0,1:T(8,128)(2,1)S(1)} collective-permute-done((bf16[512,192]{0,1:T(8,128)(2,1)S(1)}, bf16[512,192]{0,1:T(8,128)(2,1)S(1)}, u32[]{:S(2)}, u32[]{:S(2)}) %collective-permute-start.3) | collective-permute-done | bytes 196640 | tf_op jit(solution)/shard_map/ppermute | solution.py:23
  125.6 1.6 add_add_fusion
  127.6 1.4 fusion.28
  129.1 1.6 fusion.6
  130.7 28.5 %all_gather.7 = bf16[512,768]{0,1:T(8,128)(2,1)S(1)} all-gather(bf16[512,192]{0,1:T(8,128)(2,1)S(1)} %fusion.6), channel_id=1, replica_groups=mesh['bins'=128,'ch'=4] {'ch'}, dimensions={1}, use_global_device_ids=true | all-gather | bytes 983040 | tf_op jit(solution)/shard_map/all_gather | solution.py:259
  159.2 4.5 %collective-permute-start.7 = (bf16[512,768]{0,1:T(8,128)(2,1)S(1)}, bf16[512,768]{0,1:T(8,128)(2,1)S(1)}, u32[]{:S(2)}, u32[]{:S(2)}) collective-permute-start(bf16[512,768]{0,1:T(8,128)(2,1)S(1)} %all_gather.7), channel_id=1, source_target_pairs={{0,4},{4,8},{8,12},{12,16},{16,20},{20,24},{24,28},{28,32},{32,36}... | collective-permute-start | bytes 2359304 | tf_op jit(solution)/shard_map/ppermute | solution.py:23
  163.7 1.9 collective-permute-start.6
  169.4 83.3 %shard_map.75 = (bf16[3,192,768]{2,1,0:T(8,128)(2,1)S(1)}, bf16[3,192,768]{2,1,0:T(8,128)(2,1)S(1)}) custom-call(f32[3,192,768]{2,1,0:T(8,128)S(1)} %pad_maximum_fusion.near_ref, f32[3,192,768]{2,1,0:T(8,128)S(1)} %pad_maximum_fusion.1.far_ref), custom_call_target="tpu_custom_call" | custom-call | tf_op jit(solution)/shard_map/pallas_call | solution.py:214
  253.1 1.2 fusion.7
  254.3 1.7 fusion.26
  (44 shorter events, 10.3 us)
Async XLA Ops:
  7.2 9.7 %copy-start.1 = (bf16[3,192,768]{2,1,0:T(8,128)(2,1)S(1)}, bf16[3,192,768]{2,1,0:T(8,128)(2,1)}, u32[]{:S(2)}) copy-start(bf16[3,192,768]{2,1,0:T(8,128)(2,1)} %param.6) | copy-start | bytes 2654212
  7.2 105.6 %reduce-scatter.3.cloned.1.call-start = ((), (), s32[]{:S(2)}) async-start(), calls=%async_computation.2 | async-start | bytes 1966080 | tf_op jit(solution)/shard_map/reduce_scatter | solution.py:250
  8.4 8.5 %collective-permute-start = (bf16[512,192]{0,1:T(8,128)(2,1)S(1)}, bf16[512,192]{0,1:T(8,128)(2,1)S(1)}, u32[]{:S(2)}, u32[]{:S(2)}) collective-permute-start(bf16[512,192]{0,1:T(8,128)(2,1)S(1)} %fusion.16), channel_id=1, source_target_pairs={{0,4},{4,8},{8,12},{12,16},{16,20},{20,24},{24,28},{28,32},{32,36}... | collective-permute-start | bytes 589832 | tf_op jit(solution)/shard_map/ppermute | solution.py:23
  11.8 10.4 %collective-permute-start.1 = (bf16[512,192]{0,1:T(8,128)(2,1)S(1)}, bf16[512,192]{0,1:T(8,128)(2,1)S(1)}, u32[]{:S(2)}, u32[]{:S(2)}) collective-permute-start(bf16[512,192]{0,1:T(8,128)(2,1)S(1)} %fusion.16), channel_id=1, source_target_pairs={{4,0},{8,4},{12,8},{16,12},{20,16},{24,20},{28,24},{32,28},{36,32}... | collective-permute-start | bytes 589832 | tf_op jit(solution)/shard_map/ppermute | solution.py:23
  16.9 5.2 %copy-start.3 = (bf16[512,192]{0,1:T(8,128)(2,1)}, bf16[512,192]{0,1:T(8,128)(2,1)S(1)}, u32[]{:S(2)}) copy-start(bf16[512,192]{0,1:T(8,128)(2,1)S(1)} %collective-permute-done) | copy-start | bytes 589828
  23.7 0.9 copy-start.7
  23.7 89.0 %copy-start.2 = (bf16[512,192]{0,1:T(8,128)(2,1)S(1)}, bf16[512,192]{0,1:T(8,128)(2,1)}, u32[]{:S(2)}) copy-start(bf16[512,192]{0,1:T(8,128)(2,1)} %param.4) | copy-start | bytes 589828
  23.7 94.9 %copy-start = (bf16[3,192,768]{2,1,0:T(8,128)(2,1)S(1)}, bf16[3,192,768]{2,1,0:T(8,128)(2,1)}, u32[]{:S(2)}) copy-start(bf16[3,192,768]{2,1,0:T(8,128)(2,1)} %param.7) | copy-start | bytes 2654212
  23.8 230.5 %reduce-scatter.5.cloned.1.call-start = ((), (), s32[]{:S(2)}) async-start(), calls=%async_computation.3 | async-start | bytes 1966080 | tf_op jit(solution)/shard_map/reduce_scatter | solution.py:250
  45.9 81.7 %collective-permute-start.5 = (bf16[512,768]{0,1:T(8,128)(2,1)S(1)}, bf16[512,768]{0,1:T(8,128)(2,1)}, u32[]{:S(2)}, u32[]{:S(2)}) collective-permute-start(bf16[512,768]{0,1:T(8,128)(2,1)S(1)} %all_gather.6), channel_id=1, source_target_pairs={{0,16},{4,20},{8,24},{12,28},{16,32},{20,36},{24,40},{28,44},{32,4... | collective-permute-start | bytes 2359304 | tf_op jit(solution)/shard_map/ppermute | solution.py:23
  50.2 78.8 %collective-permute-start.4 = (bf16[512,768]{0,1:T(8,128)(2,1)S(1)}, bf16[512,768]{0,1:T(8,128)(2,1)}, u32[]{:S(2)}, u32[]{:S(2)}) collective-permute-start(bf16[512,768]{0,1:T(8,128)(2,1)S(1)} %all_gather.6), channel_id=1, source_target_pairs={{16,0},{20,4},{24,8},{28,12},{32,16},{36,20},{40,24},{44,28},{48,3... | collective-permute-start | bytes 2359304 | tf_op jit(solution)/shard_map/ppermute | solution.py:23
  113.9 7.6 %collective-permute-start.2 = (bf16[512,192]{0,1:T(8,128)(2,1)S(1)}, bf16[512,192]{0,1:T(8,128)(2,1)S(1)}, u32[]{:S(2)}, u32[]{:S(2)}) collective-permute-start(bf16[512,192]{0,1:T(8,128)(2,1)S(1)} %get-tuple-element.8), channel_id=1, source_target_pairs={{0,16},{4,20},{8,24},{12,28},{16,32},{20,36},{24,40},{28,44},{32,4... | collective-permute-start | bytes 589832 | tf_op jit(solution)/shard_map/ppermute | solution.py:23
  117.3 8.3 %collective-permute-start.3 = (bf16[512,192]{0,1:T(8,128)(2,1)S(1)}, bf16[512,192]{0,1:T(8,128)(2,1)S(1)}, u32[]{:S(2)}, u32[]{:S(2)}) collective-permute-start(bf16[512,192]{0,1:T(8,128)(2,1)S(1)} %get-tuple-element.8), channel_id=1, source_target_pairs={{16,0},{20,4},{24,8},{28,12},{32,16},{36,20},{40,24},{44,28},{48,3... | collective-permute-start | bytes 589832 | tf_op jit(solution)/shard_map/ppermute | solution.py:23
  121.5 0.7 copy-start.5
  127.3 1.8 copy-start.8
  159.2 93.5 %collective-permute-start.7 = (bf16[512,768]{0,1:T(8,128)(2,1)S(1)}, bf16[512,768]{0,1:T(8,128)(2,1)S(1)}, u32[]{:S(2)}, u32[]{:S(2)}) collective-permute-start(bf16[512,768]{0,1:T(8,128)(2,1)S(1)} %all_gather.7), channel_id=1, source_target_pairs={{0,4},{4,8},{8,12},{12,16},{16,20},{20,24},{24,28},{28,32},{32,36}... | collective-permute-start | bytes 2359304 | tf_op jit(solution)/shard_map/ppermute | solution.py:23
  163.7 89.4 %collective-permute-start.6 = (bf16[512,768]{0,1:T(8,128)(2,1)S(1)}, bf16[512,768]{0,1:T(8,128)(2,1)S(1)}, u32[]{:S(2)}, u32[]{:S(2)}) collective-permute-start(bf16[512,768]{0,1:T(8,128)(2,1)S(1)} %all_gather.7), channel_id=1, source_target_pairs={{4,0},{8,4},{12,8},{16,12},{20,16},{24,20},{28,24},{32,28},{36,32}... | collective-permute-start | bytes 2359304 | tf_op jit(solution)/shard_map/ppermute | solution.py:23
  166.5 0.9 copy-start.4
  168.0 0.9 copy-start.6
Sparse Core Ops, SparseCore 0:
  23.9 88.8 reduce-scatter.2
  127.4 84.4 reduce-scatter.4

commit v2 on v0

v2 whole, which is shorter than its diff:
```python
import math

import jax
import jax.numpy as jnp
from jax import lax
from jax.experimental import pallas as pl
from jax.experimental.pallas import tpu as pltpu
from jax.sharding import PartitionSpec as P

MESH = pl.DeviceIdType.MESH
ROWS = 512
CHUNKS = 4
CHUNK = ROWS // CHUNKS
UNITS = 27
LAST_BIN = 127
BINS = 65536
F32, BF16 = jnp.float32, jnp.bfloat16

gelu_coeff = 0.7978845608

AXES = (("x", "y"), ("y", "x"))


def gelu_value(values):
    inner = gelu_coeff * (values + 0.044715 * values * values * values)
    return 0.5 * values * (1.0 + jnp.tanh(inner))


def gelu_slope(values):
    inner = gelu_coeff * (values + 0.044715 * values * values * values)
    tangent = jnp.tanh(inner)
    return 0.5 * (1.0 + tangent) + 0.5 * values * (1.0 - tangent * tangent) * gelu_coeff * (
        1.0 + 3.0 * 0.044715 * values * values
    )


def product(left, right):
    return jnp.dot(left, right, preferred_element_type=F32)


def against(left, right):
    return lax.dot_general(left, right, (((1,), (1,)), ((), ())), preferred_element_type=F32)


def over_rows(left, right):
    return lax.dot_general(left, right, (((0,), (0,)), ((), ())), preferred_element_type=F32)


class Place:
    def __init__(self):
        b = lax.axis_index("bins")
        self.b = b
        self.ch = lax.axis_index("ch")
        self.half = lax.div(self.ch, 2)
        self.core = lax.rem(self.ch, 2)
        self.x = lax.rem(b, 4)
        self.y = lax.rem(lax.div(b, 4), 4)
        self.z = lax.div(b, 16)
        self.other_half = (b, lax.rem(self.ch + 2, 4))
        self.other_core = (b, self.half * 2 + 1 - self.core)

    def shifted(self, axis, d):
        x, y, z = self.x, self.y, self.z
        if axis == "x":
            x = lax.rem(x + d, 4)
        elif axis == "y":
            y = lax.rem(y + d, 4)
        else:
            z = lax.rem(z + d, 8)
        return (z * 16 + y * 4 + x, self.ch)

    def along(self, distance):
        return (lax.rem(self.b + distance + 128, 128), self.ch)

    def coordinate(self, axis):
        return {"x": self.x, "y": self.y, "z": self.z}[axis]


def remote(src, dst, send_sem, recv_sem, target):
    return pltpu.make_async_remote_copy(
        src_ref=src,
        dst_ref=dst,
        send_sem=send_sem,
        recv_sem=recv_sem,
        device_id=target,
        device_id_type=MESH,
    )


class Sender:
    def __init__(self):
        self.pending = []

    def __call__(self, src, dst, sems, index, target):
        copy = remote(src, dst, sems[0].at[index], sems[1].at[index], target)
        copy.start()
        self.pending.append((None, copy))
        return copy

    def when(self, condition, src, dst, sems, index, target):
        copy = remote(src, dst, sems[0].at[index], sems[1].at[index], target)

        @pl.when(condition)
        def _():
            copy.start()

        self.pending.append((condition, copy))
        return copy

    def finish(self):
        for condition, copy in self.pending:
            if condition is None:
                copy.wait_send()
            else:
                pl.when(condition)(copy.wait_send)


def kernel(x_ref, c_ref, w1_ref, w2_ref, act_out, grad_out, near_out, far_out, *scratch):
    s = dict(zip(SCRATCH, scratch))
    me = Place()
    half, core = me.half, me.core
    send = Sender()
    barrier = pltpu.get_barrier_semaphore()

    def sems(name):
        return s[name + "_s"], s[name + "_r"]

    def neighbours(hops):
        return me.b >= hops, me.b <= LAST_BIN - hops

    near_low, near_high = neighbours(1)
    far_low, far_high = neighbours(4)

    for axis, n in (("x", 4), ("y", 4), ("z", 8)):
        for d in range(1, n):
            pl.semaphore_signal(barrier, inc=1, device_id=me.shifted(axis, d), device_id_type=MESH)
    pl.semaphore_signal(barrier, inc=1, device_id=me.other_half, device_id_type=MESH)
    pl.semaphore_signal(barrier, inc=1, device_id=me.other_core, device_id_type=MESH)
    for hops, condition in ((-1, near_low), (1, near_high), (-4, far_low), (4, far_high)):

        @pl.when(condition)
        def _(hops=hops):
            pl.semaphore_signal(barrier, inc=1, device_id=me.along(hops), device_id_type=MESH)

    x0p, u1, x1p, u2, g2, g1 = (s[n] for n in ("x0p", "u1", "x1p", "u2", "g2", "g1"))

    def blank(condition, ref):
        @pl.when(jnp.logical_not(condition))
        def _():
            ref[...] = jnp.zeros(ref.shape, ref.dtype)

    blank(near_low, u1.at[0])
    blank(near_high, u1.at[2])
    blank(far_low, u2.at[0])
    blank(far_high, u2.at[2])

    @pl.when(jnp.logical_not(far_high))
    def _():
        g2[0, core] = jnp.zeros((ROWS, 384), BF16)

    @pl.when(jnp.logical_not(far_low))
    def _():
        g2[2, core] = jnp.zeros((ROWS, 384), BF16)

    @pl.when(jnp.logical_not(near_high))
    def _():
        g1[0, core] = jnp.zeros((ROWS, 384), BF16)

    @pl.when(jnp.logical_not(near_low))
    def _():
        g1[2, core] = jnp.zeros((ROWS, 384), BF16)

    def pack(ref, packed, main_at, tail_at):
        for m in range(CHUNKS):
            top = m * CHUNK
            packed[m, :CHUNK] = ref[top : top + CHUNK, main_at : main_at + 128]
            upper = ref[top : top + 64, tail_at : tail_at + 64]
            lower = ref[top + 64 : top + 128, tail_at : tail_at + 64]
            packed[m, CHUNK:] = jnp.concatenate([upper, lower], axis=1)

    @pl.when(core == 0)
    def _():
        pack(x_ref, s["xs"], 0, 128)
        pack(c_ref, s["cs"], 0, 128)

    @pl.when(core == 1)
    def _():
        pack(x_ref, s["xs"], 64, 0)
        pack(c_ref, s["cs"], 64, 0)

    wires = 15 + sum(c.astype(jnp.int32) for c in (near_low, near_high, far_low, far_high))
    pl.semaphore_wait(barrier, wires)

    weights = (w1_ref, w2_ref)
    parts = [(b, p) for b in (0, 1) for p in (0, 1)]

    wh, we, wf = s["wh"], s["we"], s["wf"]
    crossing = {}
    for b, p in parts:
        i = 2 * b + p
        first, second = me.coordinate(AXES[p][0]), me.coordinate(AXES[p][1])
        place = lax.rem(second * 8 + me.z, UNITS)
        unit = p * 108 + first * UNITS + place
        tap = lax.div(unit, 72)
        rest = lax.rem(unit, 72)
        row = pl.multiple_of(lax.div(rest, 6) * 16, 16)
        col = pl.multiple_of(lax.rem(rest, 6) * 128, 128)
        crossing[i] = send(
            weights[b].at[tap, pl.ds(row, 16), pl.ds(col, 128)], s["wu"].at[i], sems("wx"), i, me.other_half
        )
    xcopy = [send(s["xs"].at[m], s["xr"].at[m], sems("xx"), m, me.other_half) for m in range(CHUNKS)]
    ccopy = [send(s["cs"].at[m], s["cr"].at[m], sems("cx"), m, me.other_half) for m in range(CHUNKS)]

    def gather_lines(i, grouped, name):
        return [
            send(grouped.at[i, me.z], grouped.at[i, me.z], sems(name), (i, d - 1), me.shifted("z", d))
            for d in range(1, 8)
        ]

    def gather_second(i, p, grouped, wide, name):
        axis = AXES[p][1]
        there = pl.ds(me.coordinate(axis) * 8, 8)
        copies = [
            send(grouped.at[i], wide.at[i, there], sems(name), (i, d - 1), me.shifted(axis, d)) for d in (1, 2, 3)
        ]
        wide[i, there] = grouped[i]
        return copies

    def gather_first(b, p, wide, whole, name):
        axis = AXES[p][0]
        i = 2 * b + p
        here = pl.ds(p * 108 + me.coordinate(axis) * UNITS, UNITS)
        copies = [
            send(wide.at[i, pl.ds(0, UNITS)], whole.at[b, here], sems(name), (i, d - 1), me.shifted(axis, d))
            for d in (1, 2, 3)
        ]
        whole[b, here] = wide[i, :UNITS]
        return copies

    def arrived(copies):
        for copy in copies:
            copy.wait_recv()

    def paired(mine, theirs):
        own = mine[CHUNK:].astype(F32)
        other = theirs[CHUNK:].astype(F32)
        low = jnp.where(half == 0, own, other)
        high = jnp.where(half == 0, other, own)
        upper = jnp.concatenate([low[:, :64], high[:, :64]], axis=1)
        lower = jnp.concatenate([low[:, 64:], high[:, 64:]], axis=1)
        own_main = mine[:CHUNK].astype(F32)
        other_main = theirs[:CHUNK].astype(F32)
        return (
            jnp.where(half == 0, own_main, other_main),
            jnp.where(half == 0, other_main, own_main),
            jnp.concatenate([upper, lower], axis=0),
        )

    near_copies = []
    far_u_copies = []

    def x_chunk(m):
        xcopy[m].wait_recv()
        rows = pl.ds(m * CHUNK, CHUNK)
        for t, tile in enumerate(paired(s["xs"].at[m], s["xr"].at[m])):
            x0p[rows, t * 128 : (t + 1) * 128] = tile.astype(BF16)
            u1[1, rows, t * 128 : (t + 1) * 128] = gelu_value(tile).astype(BF16)
        low = send.when(near_low, u1.at[1, rows], u1.at[2, rows], sems("u1h"), (0, m), me.along(-1))
        high = send.when(near_high, u1.at[1, rows], u1.at[0, rows], sems("u1h"), (1, m), me.along(1))
        near_copies.append((near_high, low))
        near_copies.append((near_low, high))

    g2_copies, g2_core = [], []

    def c_chunk(m):
        ccopy[m].wait_recv()
        rows = pl.ds(m * CHUNK, CHUNK)
        for t, tile in enumerate(paired(s["cs"].at[m], s["cr"].at[m])):
            g2[1, core, rows, t * 128 : (t + 1) * 128] = tile.astype(BF16)
        mine = g2.at[1, core, rows]
        low = send.when(far_low, mine, g2.at[0, core, rows], sems("g2h"), (0, m), me.along(-4))
        high = send.when(far_high, mine, g2.at[2, core, rows], sems("g2h"), (1, m), me.along(4))
        g2_copies.append((far_high, low))
        g2_copies.append((far_low, high))
        g2_core.append(send(mine, g2.at[1, core, rows], sems("g2c"), m, me.other_core))

    def halo_arrived(copies):
        for condition, copy in copies:
            pl.when(condition)(copy.wait_recv)

    x_chunk(0)
    lines, seconds, firsts = {}, {}, {}
    for b, p in parts:
        i = 2 * b + p
        crossing[i].wait_recv()
        wh[i, me.z] = s["wu"][i]
        lines[i] = gather_lines(i, wh, "wz")
    x_chunk(1)
    for b, p in parts:
        i = 2 * b + p
        arrived(lines[i])
        seconds[i] = gather_second(i, p, wh, we, "w2")
    x_chunk(2)
    for b, p in parts:
        i = 2 * b + p
        arrived(seconds[i])
        firsts[i] = gather_first(b, p, we, wf, "w1")
    x_chunk(3)
    c_chunk(0)

    def assemble(b, out):
        ref = weights[b]
        own_main, own_tail = half * 128, 256 + half * 64
        other_main, other_tail = 128 - half * 128, 320 - half * 64

        def columns(tiles):
            low, high = tiles[1], tiles[4]
            return (
                tiles[0],
                tiles[3],
                jnp.concatenate([low[:, :64], high[:, :64]], axis=1),
                tiles[2],
                tiles[5],
                jnp.concatenate([low[:, 64:], high[:, 64:]], axis=1),
            )

        def step(k, _):
            tap, i = lax.div(k, 12), lax.rem(k, 12)
            natural = lax.rem(i + 4 * core, 12)
            tail = i >= 8
            own_at = jnp.where(tail, own_tail + (i - 8) * 16, own_main + i * 16)
            other_at = jnp.where(tail, other_tail + (i - 8) * 16, other_main + i * 16)
            own_at, other_at = pl.multiple_of(own_at, 16), pl.multiple_of(other_at, 16)
            rows = pl.ds(pl.multiple_of(natural * 16, 16), 16)
            own = columns([ref[tap, rows, t * 128 : (t + 1) * 128] for t in range(6)])
            other = columns([wf[b, tap * 72 + natural * 6 + t] for t in range(6)])
            for t in range(6):
                out[tap, pl.ds(own_at, 16), t * 128 : (t + 1) * 128] = own[t]
                out[tap, pl.ds(other_at, 16), t * 128 : (t + 1) * 128] = other[t]
            return 0

        lax.fori_loop(0, 36, step, 0)

    arrived(firsts[0])
    arrived(firsts[1])
    assemble(0, s["wp1"])
    c_chunk(1)
    halo_arrived(near_copies)

    wp1, wp2 = s["wp1"], s["wp2"]
    zs, zo, zr = s["zs"], s["zo"], s["zr"]

    def conv(taps, weight, columns, out):
        width = columns.size

        def step(m, _):
            rows = pl.ds(m * CHUNK, CHUNK)
            total = product(taps[0, rows], weight[0, :, columns])
            total = total + product(taps[1, rows], weight[1, :, columns])
            out[rows, :width] = total + product(taps[2, rows], weight[2, :, columns])
            return 0

        lax.fori_loop(0, CHUNKS, step, 0)

    def pair_columns(which):
        return pl.ds(pl.multiple_of(which * 384, 128), 384)

    conv(u1, wp1, pair_columns(1 - core), zs)
    z1_copy = send(zs, zr, sems("z1"), 0, me.other_core)
    conv(u1, wp1, pair_columns(core), zo)
    z1_copy.wait_recv()

    def first_out(m, _):
        rows = pl.ds(m * CHUNK, CHUNK)
        value = x0p[rows].astype(F32) + (zo[rows] + zr[rows])
        rounded = value.astype(BF16)
        x1p[rows] = rounded
        u2[1, rows] = gelu_value(rounded.astype(F32)).astype(BF16)
        return 0

    u2_copies = []
    for m in range(CHUNKS):
        first_out(m, 0)
        rows = pl.ds(m * CHUNK, CHUNK)
        low = send.when(far_low, u2.at[1, rows], u2.at[2, rows], sems("u2h"), (0, m), me.along(-4))
        high = send.when(far_high, u2.at[1, rows], u2.at[0, rows], sems("u2h"), (1, m), me.along(4))
        u2_copies.append((far_high, low))
        u2_copies.append((far_low, high))
    c_chunk(2)
    c_chunk(3)
    arrived(firsts[2])
    arrived(firsts[3])
    assemble(1, wp2)

    def spread(full, name):
        return [send(full.at[t, core], full.at[t, core], sems(name), t, me.other_core) for t in (0, 2)]

    halo_arrived(g2_copies)
    g2_spread = spread(g2, "g2s")
    arrived(g2_core)

    d1, r1, d2, r2, d3, r3 = (s[n] for n in ("d1", "r1", "d2", "r2", "d3", "r3"))

    def weight_grad(b, taps, full):
        def step(tap, _):
            main = taps[tap, :, pl.ds(pl.multiple_of(half * 128, 128), 128)]
            tails = taps[tap, :, 256:384].astype(F32)
            tail = jnp.where(half == 0, tails[:, :64], tails[:, 64:]).astype(BF16)
            for c in (0, 1):
                upper = over_rows(main, full[1, c]).astype(BF16)
                lower = over_rows(tail, full[1, c]).astype(BF16)
                for t in range(3):
                    for i in range(8):
                        d1[b, tap * 72 + i * 6 + c * 3 + t] = upper[i * 16 : i * 16 + 16, t * 128 : t * 128 + 128]
                    for i in range(4):
                        d1[b, tap * 72 + (8 + i) * 6 + c * 3 + t] = lower[
                            i * 16 : i * 16 + 16, t * 128 : t * 128 + 128
                        ]
            return 0

        lax.fori_loop(0, 3, step, 0)

    def reduce_first(b, p):
        i = 2 * b + p
        axis = AXES[p][0]
        here = me.coordinate(axis)
        return [
            send(
                d1.at[b, pl.ds(p * 108 + lax.rem(here + d, 4) * UNITS, UNITS)],
                r1.at[i, d - 1],
                sems("s1"),
                (i, d - 1),
                me.shifted(axis, d),
            )
            for d in (1, 2, 3)
        ]

    def reduce_second(b, p, copies):
        i = 2 * b + p
        arrived(copies)
        base = p * 108 + me.coordinate(AXES[p][0]) * UNITS

        def step(r, _):
            total = d1[b, pl.ds(base + r * 9, 9)].astype(F32)
            for d in range(3):
                total = total + r1[i, d, pl.ds(r * 9, 9)].astype(F32)
            d2[i, pl.ds(r * 9, 9)] = total.astype(BF16)
            return 0

        lax.fori_loop(0, 3, step, 0)
        d2[i, UNITS:] = jnp.zeros((32 - UNITS, 16, 128), BF16)
        axis = AXES[p][1]
        there = me.coordinate(axis)
        return [
            send(
                d2.at[i, pl.ds(lax.rem(there + d, 4) * 8, 8)], r2.at[i, d - 1], sems("s2"), (i, d - 1),
                me.shifted(axis, d),
            )
            for d in (1, 2, 3)
        ]

    def reduce_third(b, p, copies):
        i = 2 * b + p
        arrived(copies)
        there = me.coordinate(AXES[p][1])
        total = d2[i, pl.ds(there * 8, 8)].astype(F32)
        for d in range(3):
            total = total + r2[i, d].astype(F32)
        d3[i] = total.astype(BF16)
        return [
            send(d3.at[i, lax.rem(me.z + d, 8)], r3.at[i, d - 1], sems("s3"), (i, d - 1), me.shifted("z", d))
            for d in range(1, 8)
        ]

    gh, ge, gf = s["gh"], s["ge"], s["gf"]

    def reduced(b, p, copies):
        i = 2 * b + p
        arrived(copies)
        total = d3[i, me.z].astype(F32)
        for d in range(7):
            total = total + r3[i, d].astype(F32)
        gh[i, me.z] = (total * (1.0 / math.sqrt(BINS))).astype(BF16)
        return gather_lines(i, gh, "gz")

    arrived(g2_spread)
    v = s["v"]

    def back_two(m, _):
        rows = pl.ds(m * CHUNK, CHUNK)
        total = jnp.zeros((CHUNK, 384), F32)
        for tap in range(3):
            for c in (0, 1):
                total = total + against(g2[tap, c, rows], wp2[tap, :, c * 384 : (c + 1) * 384])
        previous = x1p[rows].astype(F32)
        g1[1, core, rows] = (g2[1, core, rows].astype(F32) + gelu_slope(previous) * total).astype(BF16)
        return 0

    g1_core, g1_copies = [], []
    for m in range(CHUNKS):
        back_two(m, 0)
        rows = pl.ds(m * CHUNK, CHUNK)
        g1_core.append(send(g1.at[1, core, rows], g1.at[1, core, rows], sems("g1c"), m, me.other_core))
    arrived(g1_core)
    weight_grad(0, u1, g1)
    reduce = {}
    for p in (0, 1):
        reduce[0, p] = reduce_first(0, p)
    halo_arrived(u2_copies)
    weight_grad(1, u2, g2)
    for p in (0, 1):
        reduce[1, p] = reduce_first(1, p)
    for m in range(CHUNKS):
        rows = pl.ds(m * CHUNK, CHUNK)
        mine = g1.at[1, core, rows]
        low = send.when(near_low, mine, g1.at[0, core, rows], sems("g1h"), (0, m), me.along(-1))
        high = send.when(near_high, mine, g1.at[2, core, rows], sems("g1h"), (1, m), me.along(1))
        g1_copies.append((near_high, low))
        g1_copies.append((near_low, high))

    def own_columns(which):
        return pl.ds(pl.multiple_of(which * 384 + half * 128, 128), 128), pl.ds(
            pl.multiple_of(which * 384 + 256, 128), 128
        )

    ys, yo, yr = s["ys"], s["yo"], s["yr"]

    def conv_own(which, out):
        main, tails = own_columns(which)

        def step(m, _):
            rows = pl.ds(m * CHUNK, CHUNK)
            for at, columns in ((0, main), (128, tails)):
                total = product(u2[0, rows], wp2[0, :, columns])
                total = total + product(u2[1, rows], wp2[1, :, columns])
                out[rows, at : at + 128] = total + product(u2[2, rows], wp2[2, :, columns])
            return 0

        lax.fori_loop(0, CHUNKS, step, 0)

    conv_own(1 - core, ys)
    z2_copy = send(ys, yr, sems("z2"), 0, me.other_core)
    conv_own(core, yo)
    z2_copy.wait_recv()

    main_tile = pl.ds(pl.multiple_of(half * 128, 128), 128)

    def own_tail(tile):
        return jnp.where(half == 0, tile[:, :64], tile[:, 64:])

    def put(out, rows, main, tail):
        main, tail = main.astype(BF16), tail.astype(BF16)

        @pl.when(core == 0)
        def _():
            out[rows, 0:128] = main
            out[rows, 128:192] = tail

        @pl.when(core == 1)
        def _():
            out[rows] = jnp.concatenate([tail, main], axis=1)

    def second_out(m, _):
        rows = pl.ds(m * CHUNK, CHUNK)
        main = x1p[rows, main_tile].astype(F32) + (yo[rows, 0:128] + yr[rows, 0:128])
        tails = x1p[rows, 256:384].astype(F32) + (yo[rows, 128:256] + yr[rows, 128:256])
        put(act_out, rows, main, own_tail(tails))
        return 0

    lax.fori_loop(0, CHUNKS, second_out, 0)

    for b, p in parts:
        reduce[b, p] = reduce_second(b, p, reduce[b, p])
    for b, p in parts:
        reduce[b, p] = reduce_third(b, p, reduce[b, p])
    halo_arrived(g1_copies)
    g1_spread = spread(g1, "g1s")
    for b, p in parts:
        reduce[b, p] = reduced(b, p, reduce[b, p])

    arrived(g1_spread)

    def back_one(m, _):
        rows = pl.ds(m * CHUNK, CHUNK)
        main = jnp.zeros((CHUNK, 128), F32)
        tails = jnp.zeros((CHUNK, 128), F32)
        for tap in range(3):
            for c in (0, 1):
                grad = g1[tap, c, rows]
                main = main + against(grad, wp1[tap, main_tile, c * 384 : (c + 1) * 384])
                tails = tails + against(grad, wp1[tap, 256:384, c * 384 : (c + 1) * 384])
        main = g1[1, core, rows, main_tile].astype(F32) + gelu_slope(x0p[rows, main_tile].astype(F32)) * main
        tails = g1[1, core, rows, 256:384].astype(F32) + gelu_slope(x0p[rows, 256:384].astype(F32)) * tails
        put(grad_out, rows, main, own_tail(tails))
        return 0

    lax.fori_loop(0, CHUNKS, back_one, 0)

    for b, p in parts:
        arrived(reduce[b, p])
        reduce[b, p] = gather_second(2 * b + p, p, gh, ge, "e2")
    for b, p in parts:
        arrived(reduce[b, p])
        reduce[b, p] = gather_first(b, p, ge, gf, "e1")

    def unpack(b, out):
        def step(k, _):
            tap, natural = lax.div(k, 12), lax.rem(k, 12)
            row = lax.rem(natural + 12 - 4 * core, 12)
            tiles = [gf[b, tap * 72 + row * 6 + t] for t in range(6)]
            low, high = tiles[2], tiles[5]
            ordered = (
                tiles[0],
                jnp.concatenate([low[:, :64], high[:, :64]], axis=1),
                tiles[3],
                tiles[1],
                jnp.concatenate([low[:, 64:], high[:, 64:]], axis=1),
                tiles[4],
            )
            rows = pl.ds(pl.multiple_of(natural * 16, 16), 16)
            for t in range(6):
                out[tap, rows, t * 128 : (t + 1) * 128] = ordered[t]
            return 0

        lax.fori_loop(0, 36, step, 0)

    for b, out in ((0, near_out), (1, far_out)):
        arrived(reduce[b, 0])
        arrived(reduce[b, 1])
        unpack(b, out)
    send.finish()


def buffers():
    table = {}

    def keep(name, *shape, dtype=BF16):
        table[name] = pltpu.VMEM(shape, dtype)

    def pair(name, *shape):
        table[name + "_s"] = pltpu.SemaphoreType.DMA(shape)
        table[name + "_r"] = pltpu.SemaphoreType.DMA(shape)

    for name in ("xs", "xr", "cs", "cr"):
        keep(name, CHUNKS, CHUNK + 64, 128)
    keep("x0p", ROWS, 384)
    keep("x1p", ROWS, 384)
    keep("u1", 3, ROWS, 384)
    keep("u2", 3, ROWS, 384)
    keep("g2", 3, 2, ROWS, 384)
    keep("g1", 3, 2, ROWS, 384)
    keep("wp1", 3, 384, 768)
    keep("wp2", 3, 384, 768)
    for name in ("zs", "zo", "zr", "v"):
        keep(name, ROWS, 384, dtype=F32)
    for name in ("ys", "yo", "yr"):
        keep(name, ROWS, 256, dtype=F32)
    keep("wu", 4, 16, 128)
    keep("wh", 4, 8, 16, 128)
    keep("we", 4, 32, 16, 128)
    keep("wf", 2, 216, 16, 128)
    keep("d1", 2, 216, 16, 128)
    keep("r1", 4, 3, UNITS, 16, 128)
    keep("d2", 4, 32, 16, 128)
    keep("r2", 4, 3, 8, 16, 128)
    keep("d3", 4, 8, 16, 128)
    keep("r3", 4, 7, 16, 128)
    keep("gh", 4, 8, 16, 128)
    keep("ge", 4, 32, 16, 128)
    keep("gf", 2, 216, 16, 128)
    pair("wx", 4)
    pair("xx", CHUNKS)
    pair("cx", CHUNKS)
    for name in ("wz", "gz", "s3"):
        pair(name, 4, 7)
    for name in ("w2", "w1", "s1", "s2", "e2", "e1"):
        pair(name, 4, 3)
    for name in ("u1h", "u2h", "g1h", "g2h"):
        pair(name, 2, CHUNKS)
    for name in ("g2c", "g1c"):
        pair(name, CHUNKS)
    for name in ("g2s", "g1s"):
        pair(name, 3)
    pair("z1", 1)
    pair("z2", 1)
    return table


SCRATCH = buffers()


def body(inputs, cotangent, first_kernel_weight, second_kernel_weight):
    shapes = [jax.ShapeDtypeStruct((ROWS, 192), BF16)] * 2 + [jax.ShapeDtypeStruct((3, 192, 768), BF16)] * 2
    vmem = pl.BlockSpec(memory_space=pltpu.VMEM)
    return pl.pallas_call(
        kernel,
        out_shape=tuple(shapes),
        in_specs=[vmem] * 4,
        out_specs=(vmem,) * 4,
        scratch_shapes=list(SCRATCH.values()),
        compiler_params=pltpu.CompilerParams(
            collective_id=0, has_side_effects=True, vmem_limit_bytes=56 * 2**20
        ),
    )(inputs, cotangent, first_kernel_weight, second_kernel_weight)


def solution(mesh):
    return jax.shard_map(
        body,
        mesh=mesh,
        in_specs=(P("bins", "ch"), P("bins", "ch"), P(None, "ch", None), P(None, "ch", None)),
        out_specs=(P("bins", "ch"), P("bins", "ch"), P(None, "ch", None), P(None, "ch", None)),
        check_vma=False,
    )
```

time: 2220 us -> 179 us (0.08)
  waiting for transfers between devices: 2100 us -> 0 us
  Pallas kernels: 0 us -> 169 us
  blocking collectives: 54.5 us -> 0 us
  starting transfers between devices: 32 us -> 0 us
    psum x1 -> x0, waiting for transfers between devices: 1950 us -> none  [body(): summed_near, summed_far = lax.psum((local_grads[0], local_grads[1]), 'bins')]
    pallas_call x0 -> x1, Pallas kernels: none -> 169 us  [body(): pl.pallas_call(kernel, out_shape=tuple(shapes), in_specs=[vmem] * 4, out_...]
    reduce_scatter x2 -> x0, waiting for transfers between devices: 89 us -> none  [body(): lax.psum_scatter(partial_value, 'ch', scatter_dimension=1, tiled=True)]
    all_gather x2 -> x0, blocking collectives: 54.5 us -> none  [body(): full_grad = lax.all_gather(gradient, 'ch', axis=1, tiled=True)]
    ppermute x8 -> x0, waiting for transfers between devices: 53.5 us -> none  [passed_along(): return lax.ppermute(block, axis, route)]
    ppermute x8 -> x0, starting transfers between devices: 31.9 us -> none  [passed_along(): return lax.ppermute(block, axis, route)]
  transfers between devices with their start and end apart: 11 -> 0, of which waited for: 10 -> 0; matrix products, arithmetic and copies ran while one was open for 1% -> 0% of each run, Pallas kernels for 0% -> 0%
where the time goes in v2:
time: 179 us
  Pallas kernels  169 us (94%)
  local copies, waits for them, and re-layouts  8.64 us (5%)
    pallas_call x1, Pallas kernels, body(): pl.pallas_call(kernel, out_shape=tuple(shapes), in_specs=[vmem] * 4, out_...  169 us
    unnamed x10, local copies, waits for them, and re-layouts  5.05 us
    pallas_call x2, local copies, waits for them, and re-layouts, body(): pl.pallas_call(kernel, out_shape=tuple(shapes), in_specs=[vmem] * 4, out_...  3.58 us

profile of v2, /device:TPU:6, one launch (start us, length us, event | category | flops | bytes accessed | tf_op | source)
XLA Modules:
  0.0 178.8 jit_solution(11370918783989428876)
XLA Ops:
  0.6 0.0 copy-start.2
  0.6 1.8 %copy.8.x_ref = bf16[512,192]{1,0:T(8,128)(2,1)} copy(bf16[512,192]{0,1:T(8,128)(2,1)} %param.4) | data formatting | bytes 393216 | tf_op args[0]
  2.4 0.0 copy-done.2
  2.5 0.8 copy.9.c_ref
  3.3 169.5 %shard_map.75 = (bf16[512,192]{1,0:T(8,128)(2,1)}, bf16[512,192]{1,0:T(8,128)(2,1)}, bf16[3,192,768]{2,1,0:T(8,128)(2,1)}, bf16[3,192,768]{2,1,0:T(8,128)(2,1)}) custom-call(bf16[512,192]{1,0:T(8,128)(2,1)} %copy.8.x_ref, bf16[512,192]{1,0:T(8,128)(2,1)} %copy.9.c_ref, bf16[3,192,768]{2,1,0:T(8,128)(2,1)} %w1_ref.1, bf16[3,192,768]{2,1,0:T(8,128)(2,1)} %w2_ref.1), custom_call_target="tpu_custom_call" | custom-call | tf_op jit(solution)/shard_map/pallas_call | solution.py:695
  172.8 0.0 copy-start.1
  172.8 1.8 %copy.10 = bf16[512,192]{0,1:T(8,128)(2,1)} copy(bf16[512,192]{1,0:T(8,128)(2,1)} %get-tuple-element.4) | data formatting | bytes 393216 | tf_op jit(solution)/shard_map/pallas_call | solution.py:695
  174.6 1.8 copy.11
  176.3 0.0 copy-done.1
  176.3 0.0 copy-start
  176.4 0.9 copy.14
  177.3 0.6 copy-done
  177.8 0.9 copy.15
Async XLA Ops:
  0.6 1.8 %copy-start.2 = (bf16[512,192]{0,1:T(8,128)(2,1)S(1)}, bf16[512,192]{0,1:T(8,128)(2,1)}, u32[]{:S(2)}) copy-start(bf16[512,192]{0,1:T(8,128)(2,1)} %param.5) | copy-start | bytes 589828
  172.8 3.6 %copy-start.1 = (bf16[3,192,768]{2,1,0:T(8,128)(2,1)S(1)}, bf16[3,192,768]{2,1,0:T(8,128)(2,1)}, u32[]{:S(2)}) copy-start(bf16[3,192,768]{2,1,0:T(8,128)(2,1)} %get-tuple-element.14) | copy-start | bytes 2654212
  176.3 1.5 copy-start

commit v3 on v2

v3 whole, which is shorter than its diff:
```python
import math

import jax
import jax.numpy as jnp
from jax import lax
from jax.experimental import pallas as pl
from jax.experimental.pallas import tpu as pltpu
from jax.sharding import PartitionSpec as P

MESH = pl.DeviceIdType.MESH
ROWS = 512
CHUNKS = 4
CHUNK = ROWS // CHUNKS
UNITS = 27
WINDOW = 3
LAST_BIN = 127
BINS = 65536
F32, BF16 = jnp.float32, jnp.bfloat16

gelu_coeff = 0.7978845608

AXES = (("x", "y"), ("y", "x"))


def gelu_value(values):
    inner = gelu_coeff * (values + 0.044715 * values * values * values)
    return 0.5 * values * (1.0 + jnp.tanh(inner))


def gelu_slope(values):
    inner = gelu_coeff * (values + 0.044715 * values * values * values)
    tangent = jnp.tanh(inner)
    return 0.5 * (1.0 + tangent) + 0.5 * values * (1.0 - tangent * tangent) * gelu_coeff * (
        1.0 + 3.0 * 0.044715 * values * values
    )


def product(left, right):
    return jnp.dot(left, right, preferred_element_type=F32)


def against(left, right):
    return lax.dot_general(left, right, (((1,), (1,)), ((), ())), preferred_element_type=F32)


def over_rows(left, right):
    return lax.dot_general(left, right, (((0,), (0,)), ((), ())), preferred_element_type=F32)


class Place:
    def __init__(self):
        b = lax.axis_index("bins")
        self.b = b
        self.ch = lax.axis_index("ch")
        self.half = lax.div(self.ch, 2)
        self.core = lax.rem(self.ch, 2)
        self.x = lax.rem(b, 4)
        self.y = lax.rem(lax.div(b, 4), 4)
        self.z = lax.div(b, 16)
        self.other_half = (b, lax.rem(self.ch + 2, 4))
        self.other_core = (b, self.half * 2 + 1 - self.core)

    def shifted(self, axis, d):
        x, y, z = self.x, self.y, self.z
        if axis == "x":
            x = lax.rem(x + d, 4)
        elif axis == "y":
            y = lax.rem(y + d, 4)
        else:
            z = lax.rem(z + d, 8)
        return (z * 16 + y * 4 + x, self.ch)

    def along(self, distance):
        return (lax.rem(self.b + distance + 128, 128), self.ch)

    def coordinate(self, axis):
        return {"x": self.x, "y": self.y, "z": self.z}[axis]


def remote(src, dst, send_sem, recv_sem, target):
    return pltpu.make_async_remote_copy(
        src_ref=src,
        dst_ref=dst,
        send_sem=send_sem,
        recv_sem=recv_sem,
        device_id=target,
        device_id_type=MESH,
    )


class Sender:
    def __init__(self):
        self.pending = []

    def __call__(self, src, dst, sems, index, target):
        copy = remote(src, dst, sems[0].at[index], sems[1].at[index], target)
        copy.start()
        self.pending.append((None, copy))
        return copy

    def when(self, condition, src, dst, sems, index, target):
        copy = remote(src, dst, sems[0].at[index], sems[1].at[index], target)

        @pl.when(condition)
        def _():
            copy.start()

        self.pending.append((condition, copy))
        return copy

    def finish(self):
        for condition, copy in self.pending:
            if condition is None:
                copy.wait_send()
            else:
                pl.when(condition)(copy.wait_send)


def kernel(x_ref, c_ref, w1_ref, w2_ref, act_out, grad_out, near_out, far_out, *scratch):
    s = dict(zip(SCRATCH, scratch))
    me = Place()
    half, core = me.half, me.core
    send = Sender()
    barrier = pltpu.get_barrier_semaphore()

    def sems(name):
        return s[name + "_s"], s[name + "_r"], name

    near_low, near_high = me.b >= 1, me.b <= LAST_BIN - 1
    far_low, far_high = me.b >= 4, me.b <= LAST_BIN - 4

    for axis, n in (("x", 4), ("y", 4), ("z", 8)):
        for d in range(1, n):
            pl.semaphore_signal(barrier, inc=1, device_id=me.shifted(axis, d), device_id_type=MESH)
    pl.semaphore_signal(barrier, inc=1, device_id=me.other_half, device_id_type=MESH)
    pl.semaphore_signal(barrier, inc=1, device_id=me.other_core, device_id_type=MESH)
    for hops, condition in ((-1, near_low), (1, near_high), (-4, far_low), (4, far_high)):

        @pl.when(condition)
        def _(hops=hops):
            pl.semaphore_signal(barrier, inc=1, device_id=me.along(hops), device_id_type=MESH)

    xr, u1, x1, u2, g2, g1 = (s[n] for n in ("xr", "u1", "x1", "u2", "g2", "g1"))
    OWN, OTHER = 0, 1

    def own(array, tap):
        return array.at[tap, half, core]

    def other(array, tap):
        return array.at[tap, 1 - half, core]

    def blank(condition, ref):
        @pl.when(jnp.logical_not(condition))
        def _():
            ref[...] = jnp.zeros(ref.shape, ref.dtype)

    blank(near_low, u1.at[0])
    blank(near_high, u1.at[2])
    blank(far_low, u2.at[0])
    blank(far_high, u2.at[2])
    for array, low, high in ((g2, far_low, far_high), (g1, near_low, near_high)):
        for h in (0, 1):
            blank(high, array.at[0, h, core])
            blank(low, array.at[2, h, core])

    def lanes(m):
        return pl.ds(m * CHUNK, CHUNK)

    def own_gelu(r, _):
        rows = pl.ds(pl.multiple_of(r * 16, 16), 16)
        u1[1, OWN, rows] = gelu_value(x_ref[rows].astype(F32)).astype(BF16)
        return 0

    lax.fori_loop(0, 12, own_gelu, 0)

    wires = 15 + sum(c.astype(jnp.int32) for c in (near_low, near_high, far_low, far_high))
    pl.semaphore_wait(barrier, wires)

    weights = (w1_ref, w2_ref)
    parts = [(b, p) for b in (0, 1) for p in (0, 1)]

    wh, we, wf = s["wh"], s["we"], s["wf"]
    crossing = {}
    for b, p in parts:
        i = 2 * b + p
        first, second = me.coordinate(AXES[p][0]), me.coordinate(AXES[p][1])
        place = lax.rem(second * 8 + me.z, UNITS)
        unit = p * 108 + first * UNITS + place
        tap = lax.div(unit, 72)
        rest = lax.rem(unit, 72)
        row = pl.multiple_of(lax.div(rest, 6) * 16, 16)
        col = pl.multiple_of(lax.rem(rest, 6) * 128, 128)
        crossing[i] = send(
            weights[b].at[tap, pl.ds(row, 16), pl.ds(col, 128)], s["wu"].at[i], sems("wx"), i, me.other_half
        )

    crossed = []

    def cross():
        n = len(crossed)
        if n >= 2 * CHUNKS:
            return
        m = n % CHUNKS
        if n < CHUNKS:
            crossed.append(send(x_ref.at[:, lanes(m)], xr.at[:, lanes(m)], sems("xx"), m, me.other_half))
        else:
            crossed.append(
                send(c_ref.at[:, lanes(m)], own(g2, 1).at[:, lanes(m)], sems("cx"), m, me.other_half)
            )

    for _ in range(WINDOW):
        cross()

    def halo(low, high, distance, src, low_dst, high_dst, name, index):
        down = send.when(low, src, low_dst, sems(name), (0,) + index, me.along(-distance))
        up = send.when(high, src, high_dst, sems(name), (1,) + index, me.along(distance))
        return [(high, down), (low, up)]

    def halo_arrived(copies):
        for condition, copy in copies:
            pl.when(condition)(copy.wait_recv)

    def arrived(copies):
        for copy in copies:
            copy.wait_recv()

    u1_own = halo(near_low, near_high, 1, u1.at[1, OWN], u1.at[2, OWN], u1.at[0, OWN], "u1h", (CHUNKS,))
    g2_core = [send(c_ref, own(g2, 1), sems("g2c"), CHUNKS, me.other_core)]
    g2_own = halo(far_low, far_high, 4, c_ref, own(g2, 0), own(g2, 2), "g2h", (CHUNKS,))

    def own_cotangent(r, _):
        rows = pl.ds(pl.multiple_of(r * 16, 16), 16)
        g2[1, half, core, rows] = c_ref[rows]
        return 0

    lax.fori_loop(0, 12, own_cotangent, 0)

    def gather_lines(i, grouped, name):
        return [
            send(grouped.at[i, me.z], grouped.at[i, me.z], sems(name), (i, d - 1), me.shifted("z", d))
            for d in range(1, 8)
        ]

    def gather_second(i, p, grouped, wide, name):
        axis = AXES[p][1]
        there = pl.ds(me.coordinate(axis) * 8, 8)
        copies = [
            send(grouped.at[i], wide.at[i, there], sems(name), (i, d - 1), me.shifted(axis, d)) for d in (1, 2, 3)
        ]
        wide[i, there] = grouped[i]
        return copies

    def gather_first(b, p, wide, whole, name):
        axis = AXES[p][0]
        i = 2 * b + p
        here = pl.ds(p * 108 + me.coordinate(axis) * UNITS, UNITS)
        copies = [
            send(wide.at[i, pl.ds(0, UNITS)], whole.at[b, here], sems(name), (i, d - 1), me.shifted(axis, d))
            for d in (1, 2, 3)
        ]
        whole[b, here] = wide[i, :UNITS]
        return copies

    u1_copies = []

    def x_chunk(m):
        crossed[m].wait_recv()
        cross()
        u1[1, OTHER, :, lanes(m)] = gelu_value(xr[:, lanes(m)].astype(F32)).astype(BF16)
        src = u1.at[1, OTHER, :, lanes(m)]
        u1_copies.extend(
            halo(near_low, near_high, 1, src, u1.at[2, OTHER, :, lanes(m)], u1.at[0, OTHER, :, lanes(m)], "u1h", (m,))
        )

    g2_copies = {}

    def c_chunk(m):
        crossed[CHUNKS + m].wait_recv()
        cross()
        src = other(g2, 1).at[:, lanes(m)]
        g2_copies[m] = halo(
            far_low, far_high, 4, src, other(g2, 0).at[:, lanes(m)], other(g2, 2).at[:, lanes(m)], "g2h", (m,)
        )
        g2_core.append(send(src, src, sems("g2c"), m, me.other_core))

    g2_spread = []

    def g2_forward_own():
        halo_arrived(g2_own)
        for k, tap in enumerate((0, 2)):
            g2_spread.append(send(own(g2, tap), own(g2, tap), sems("g2s"), (k, CHUNKS), me.other_core))

    def g2_forward(m):
        halo_arrived(g2_copies[m])
        for k, tap in enumerate((0, 2)):
            src = other(g2, tap).at[:, lanes(m)]
            g2_spread.append(send(src, src, sems("g2s"), (k, m), me.other_core))

    zp, zr = s["zp"], s["zr"]

    def conv_one(weight, slot, add):
        def step(n, _):
            columns = pl.ds(pl.multiple_of(n * 128, 128), 128)
            rows = pl.ds(pl.multiple_of(n * 128, 128), 128)
            total = over_rows(weight[0, :, columns], u1[0, slot])
            total = total + over_rows(weight[1, :, columns], u1[1, slot])
            total = total + over_rows(weight[2, :, columns], u1[2, slot])
            if add:
                total = total + zp[rows]
            zp[rows] = total
            return 0

        lax.fori_loop(0, 6, step, 0)

    def assemble(b, out):
        def step(k, _):
            tap, i = lax.div(k, 12), lax.rem(k, 12)
            rows = pl.ds(pl.multiple_of(i * 16, 16), 16)
            for t in range(6):
                out[tap, rows, t * 128 : (t + 1) * 128] = wf[b, k * 6 + t]
            return 0

        lax.fori_loop(0, 36, step, 0)

    wo1, wo2 = s["wo1"], s["wo2"]
    lines, seconds, firsts = {}, {}, {}
    for b, p in parts:
        i = 2 * b + p
        crossing[i].wait_recv()
        wh[i, me.z] = s["wu"][i]
        lines[i] = gather_lines(i, wh, "wz")
    x_chunk(0)
    for b, p in parts:
        i = 2 * b + p
        arrived(lines[i])
        seconds[i] = gather_second(i, p, wh, we, "w2")
    x_chunk(1)
    for b, p in parts:
        i = 2 * b + p
        arrived(seconds[i])
        firsts[i] = gather_first(b, p, we, wf, "w1")
    x_chunk(2)
    halo_arrived(u1_own)
    conv_one(w1_ref, OWN, False)
    g2_forward_own()
    x_chunk(3)
    arrived(firsts[0])
    arrived(firsts[1])
    assemble(0, wo1)
    c_chunk(0)
    halo_arrived(u1_copies)
    conv_one(wo1, OTHER, True)

    def group_rows(h, c):
        return pl.ds(pl.multiple_of((h * 2 + c) * 192, 64), 192)

    z1 = [send(zp.at[group_rows(h, 1 - core)], zr.at[h], sems("z1"), h, me.other_core) for h in (0, 1)]
    c_chunk(1)
    arrived(z1)
    u2_copies = []

    def x1_chunk(m):
        for slot, h in ((OWN, half), (OTHER, 1 - half)):
            before = x_ref[:, lanes(m)] if slot == OWN else xr[:, lanes(m)]
            total = zp[group_rows(h, core), lanes(m)] + zr[h, :, lanes(m)]
            value = (before.astype(F32) + total).astype(BF16)
            x1[slot, :, lanes(m)] = value
            u2[1, slot, :, lanes(m)] = gelu_value(value.astype(F32)).astype(BF16)
        src = u2.at[1, :, :, lanes(m)]
        u2_copies.extend(
            halo(far_low, far_high, 4, src, u2.at[2, :, :, lanes(m)], u2.at[0, :, :, lanes(m)], "u2h", (m,))
        )

    for m in range(CHUNKS):
        x1_chunk(m)
    arrived(firsts[2])
    arrived(firsts[3])
    assemble(1, wo2)
    g2_forward(0)
    c_chunk(2)
    g2_forward(1)

    v = s["v"]

    def half_columns(h):
        return pl.ds(pl.multiple_of(h * 384, 128), 384)

    arrived(g2_core[:1])
    arrived(g2_spread[:2])
    for slot, weight in ((OWN, w2_ref), (OTHER, wo2)):
        total = product(weight[0, :, half_columns(half)], g2[0, half].reshape(384, ROWS))
        total = total + product(weight[1, :, half_columns(half)], g2[1, half].reshape(384, ROWS))
        v[slot] = total + product(weight[2, :, half_columns(half)], g2[2, half].reshape(384, ROWS))
    c_chunk(3)
    g2_forward(2)
    g2_forward(3)

    d1, r1, d2, r2, d3, r3 = (s[n] for n in ("d1", "r1", "d2", "r2", "d3", "r3"))

    def weight_grad(b, left, right):
        def step(tap, _):
            for h in (0, 1):
                value = against(left(tap), right(tap, h).reshape(384, ROWS)).astype(BF16)
                for t in range(3):
                    for i in range(12):
                        d1[b, tap * 72 + i * 6 + h * 3 + t] = value[i * 16 : i * 16 + 16, t * 128 : t * 128 + 128]
            return 0

        lax.fori_loop(0, 3, step, 0)

    def reduce_first(b, p):
        i = 2 * b + p
        axis = AXES[p][0]
        here = me.coordinate(axis)
        return [
            send(
                d1.at[b, pl.ds(p * 108 + lax.rem(here + d, 4) * UNITS, UNITS)],
                r1.at[i, d - 1],
                sems("s1"),
                (i, d - 1),
                me.shifted(axis, d),
            )
            for d in (1, 2, 3)
        ]

    def reduce_second(b, p, copies):
        i = 2 * b + p
        arrived(copies)
        base = p * 108 + me.coordinate(AXES[p][0]) * UNITS

        def step(r, _):
            total = d1[b, pl.ds(base + r * 9, 9)].astype(F32)
            for d in range(3):
                total = total + r1[i, d, pl.ds(r * 9, 9)].astype(F32)
            d2[i, pl.ds(r * 9, 9)] = total.astype(BF16)
            return 0

        lax.fori_loop(0, 3, step, 0)
        d2[i, UNITS:] = jnp.zeros((32 - UNITS, 16, 128), BF16)
        axis = AXES[p][1]
        there = me.coordinate(axis)
        return [
            send(
                d2.at[i, pl.ds(lax.rem(there + d, 4) * 8, 8)], r2.at[i, d - 1], sems("s2"), (i, d - 1),
                me.shifted(axis, d),
            )
            for d in (1, 2, 3)
        ]

    def reduce_third(b, p, copies):
        i = 2 * b + p
        arrived(copies)
        there = me.coordinate(AXES[p][1])
        total = d2[i, pl.ds(there * 8, 8)].astype(F32)
        for d in range(3):
            total = total + r2[i, d].astype(F32)
        d3[i] = total.astype(BF16)
        return [
            send(d3.at[i, lax.rem(me.z + d, 8)], r3.at[i, d - 1], sems("s3"), (i, d - 1), me.shifted("z", d))
            for d in range(1, 8)
        ]

    gh, ge, gf = s["gh"], s["ge"], s["gf"]

    def reduced(b, p, copies):
        i = 2 * b + p
        arrived(copies)
        total = d3[i, me.z].astype(F32)
        for d in range(7):
            total = total + r3[i, d].astype(F32)
        gh[i, me.z] = (total * (1.0 / math.sqrt(BINS))).astype(BF16)
        return gather_lines(i, gh, "gz")

    reduce = {}
    arrived(g2_core[1:])
    arrived(g2_spread[2:])
    g1_core = []

    def back_two(n):
        wide = pl.ds(n * 256, 256)
        for slot, weight, h in ((OWN, w2_ref, half), (OTHER, wo2, 1 - half)):
            total = v[slot, :, wide]
            for tap in range(3):
                grad = g2[tap, 1 - half, :, :, wide].reshape(384, 256)
                total = total + product(weight[tap, :, half_columns(1 - half)], grad)
            slope = gelu_slope(x1[slot, :, wide].astype(F32))
            g1[1, h, core, :, wide] = (g2[1, h, core, :, wide].astype(F32) + slope * total).astype(BF16)
        src = g1.at[1, :, core, :, wide]
        g1_core.append(send(src, src, sems("g1c"), n, me.other_core))

    back_two(0)
    back_two(1)
    weight_grad(1, lambda tap: u2[1, OWN], lambda tap, h: g2[tap, h])
    for p in (0, 1):
        reduce[1, p] = reduce_first(1, p)
    arrived(g1_core)
    weight_grad(0, lambda tap: u1[tap, OWN], lambda tap, h: g1[1, h])
    for p in (0, 1):
        reduce[0, p] = reduce_first(0, p)
    src = g1.at[1, :, core]
    g1_copies = halo(near_low, near_high, 1, src, g1.at[0, :, core], g1.at[2, :, core], "g1h", (0,))

    yp, yr = s["yp"], s["yr"]

    def conv_two(n, _):
        columns = pl.ds(pl.multiple_of(half * 384 + n * 128, 128), 128)
        total = jnp.zeros((128, ROWS), F32)
        for tap in range(3):
            total = total + over_rows(w2_ref[tap, :, columns], u2[tap, OWN])
            total = total + over_rows(wo2[tap, :, columns], u2[tap, OTHER])
        yp[pl.ds(pl.multiple_of(n * 128, 128), 128)] = total
        return 0

    order = [(b, p) for b in (1, 0) for p in (0, 1)]
    halo_arrived(u2_copies)
    lax.fori_loop(0, 3, conv_two, 0)
    z2 = send(yp.at[pl.ds(pl.multiple_of((1 - core) * 192, 64), 192)], yr, sems("z2"), 0, me.other_core)
    for b, p in order:
        reduce[b, p] = reduce_second(b, p, reduce[b, p])
    z2.wait_recv()
    for m in range(CHUNKS):
        total = yp[pl.ds(pl.multiple_of(core * 192, 64), 192), lanes(m)] + yr[:, lanes(m)]
        act_out[:, lanes(m)] = (x1[OWN, :, lanes(m)].astype(F32) + total).astype(BF16)
    for b, p in order:
        reduce[b, p] = reduce_third(b, p, reduce[b, p])
    halo_arrived(g1_copies)
    g1_spread = [send(g1.at[t, :, core], g1.at[t, :, core], sems("g1s"), k, me.other_core) for k, t in ((0, 0), (1, 2))]
    for b, p in order:
        reduce[b, p] = reduced(b, p, reduce[b, p])

    arrived(g1_spread)

    for n in (0, 1):
        wide = pl.ds(n * 256, 256)
        total = product(w1_ref[0], g1[0, :, :, :, wide].reshape(768, 256))
        total = total + product(w1_ref[1], g1[1, :, :, :, wide].reshape(768, 256))
        total = total + product(w1_ref[2], g1[2, :, :, :, wide].reshape(768, 256))
        slope = gelu_slope(x_ref[:, wide].astype(F32))
        grad_out[:, wide] = (g1[1, half, core, :, wide].astype(F32) + slope * total).astype(BF16)

    for b, p in order:
        arrived(reduce[b, p])
        reduce[b, p] = gather_second(2 * b + p, p, gh, ge, "e2")
    for b, p in order:
        arrived(reduce[b, p])
        reduce[b, p] = gather_first(b, p, ge, gf, "e1")

    def unpack(b, out):
        def step(k, _):
            tap, i = lax.div(k, 12), lax.rem(k, 12)
            rows = pl.ds(pl.multiple_of(i * 16, 16), 16)
            for t in range(6):
                out[tap, rows, t * 128 : (t + 1) * 128] = gf[b, k * 6 + t]
            return 0

        lax.fori_loop(0, 36, step, 0)

    for b, out in ((1, far_out), (0, near_out)):
        arrived(reduce[b, 0])
        arrived(reduce[b, 1])
        unpack(b, out)
    send.finish()


def buffers():
    table = {}

    def keep(name, *shape, dtype=BF16):
        table[name] = pltpu.VMEM(shape, dtype)

    def pair(name, *shape):
        table[name + "_s"] = pltpu.SemaphoreType.DMA(shape)
        table[name + "_r"] = pltpu.SemaphoreType.DMA(shape)

    keep("xr", 192, ROWS)
    keep("x1", 2, 192, ROWS)
    keep("u1", 3, 2, 192, ROWS)
    keep("u2", 3, 2, 192, ROWS)
    keep("g2", 3, 2, 2, 192, ROWS)
    keep("g1", 3, 2, 2, 192, ROWS)
    keep("wo1", 3, 192, 768)
    keep("wo2", 3, 192, 768)
    keep("zp", 768, ROWS, dtype=F32)
    keep("zr", 2, 192, ROWS, dtype=F32)
    keep("v", 2, 192, ROWS, dtype=F32)
    keep("yp", 384, ROWS, dtype=F32)
    keep("yr", 192, ROWS, dtype=F32)
    keep("wu", 4, 16, 128)
    keep("wh", 4, 8, 16, 128)
    keep("we", 4, 32, 16, 128)
    keep("wf", 2, 216, 16, 128)
    keep("d1", 2, 216, 16, 128)
    keep("r1", 4, 3, UNITS, 16, 128)
    keep("d2", 4, 32, 16, 128)
    keep("r2", 4, 3, 8, 16, 128)
    keep("d3", 4, 8, 16, 128)
    keep("r3", 4, 7, 16, 128)
    keep("gh", 4, 8, 16, 128)
    keep("ge", 4, 32, 16, 128)
    keep("gf", 2, 216, 16, 128)
    pair("wx", 4)
    pair("xx", CHUNKS)
    pair("cx", CHUNKS)
    for name in ("wz", "gz", "s3"):
        pair(name, 4, 7)
    for name in ("w2", "w1", "s1", "s2", "e2", "e1"):
        pair(name, 4, 3)
    for name in ("u1h", "g2h", "g2s"):
        pair(name, 2, CHUNKS + 1)
    pair("u2h", 2, CHUNKS)
    pair("g1h", 2, 1)
    pair("g2c", CHUNKS + 1)
    for name in ("g1c", "g1s", "z1"):
        pair(name, 2)
    pair("z2", 1)
    return table


SCRATCH = buffers()


def body(inputs, cotangent, first_kernel_weight, second_kernel_weight):
    shapes = [jax.ShapeDtypeStruct((192, ROWS), BF16)] * 2 + [jax.ShapeDtypeStruct((3, 192, 768), BF16)] * 2
    vmem = pl.BlockSpec(memory_space=pltpu.VMEM)
    act, grad, near, far = pl.pallas_call(
        kernel,
        out_shape=tuple(shapes),
        in_specs=[vmem] * 4,
        out_specs=(vmem,) * 4,
        scratch_shapes=list(SCRATCH.values()),
        compiler_params=pltpu.CompilerParams(
            collective_id=0, has_side_effects=True, vmem_limit_bytes=56 * 2**20
        ),
    )(inputs.T, cotangent.T, first_kernel_weight, second_kernel_weight)
    return act.T, grad.T, near, far


def solution(mesh):
    return jax.shard_map(
        body,
        mesh=mesh,
        in_specs=(P("bins", "ch"), P("bins", "ch"), P(None, "ch", None), P(None, "ch", None)),
        out_specs=(P("bins", "ch"), P("bins", "ch"), P(None, "ch", None), P(None, "ch", None)),
        check_vma=False,
    )
```

time: 179 us -> 155 us (0.87)
  Pallas kernels: 169 us -> 148 us
  local copies, waits for them, and re-layouts: 8.64 us -> 5.47 us
    pallas_call x1, Pallas kernels: 169 us -> 148 us  [body(): pl.pallas_call(kernel, out_shape=tuple(shapes), in_specs=[vmem] * 4, out_...]
    pallas_call x2 -> x0, local copies, waits for them, and re-layouts: 3.58 us -> none  [body(): pl.pallas_call(kernel, out_shape=tuple(shapes), in_specs=[vmem] * 4, out_...]
    unnamed x10 -> x8, local copies, waits for them, and re-layouts: 5.05 us -> 5.47 us
where the time goes in v3:
time: 155 us; the launch traced here: 154 us
  Pallas kernels  148 us (95%)
  local copies, waits for them, and re-layouts  5.47 us (4%)
    pallas_call x1, Pallas kernels, body(): pl.pallas_call(kernel, out_shape=tuple(shapes), in_specs=[vmem] * 4, out_...  148 us
    unnamed x8, local copies, waits for them, and re-layouts  5.47 us

profile of v3, /device:TPU:6, one launch (start us, length us, event | category | flops | bytes accessed | tf_op | source)
XLA Modules:
  0.0 153.8 jit_solution(2996063328072764036)
XLA Ops:
  0.6 147.6 %shard_map.75 = (bf16[192,512]{1,0:T(8,128)(2,1)}, bf16[192,512]{1,0:T(8,128)(2,1)}, bf16[3,192,768]{2,1,0:T(8,128)(2,1)}, bf16[3,192,768]{2,1,0:T(8,128)(2,1)}) custom-call(bf16[192,512]{1,0:T(8,128)(2,1)} %bitcast.4, bf16[192,512]{1,0:T(8,128)(2,1)} %bitcast.5, bf16[3,192,768]{2,1,0:T(8,128)(2,1)} %w1_ref.1, bf16[3,192,768]{2,1,0:T(8,128)(2,1)} %w2_ref.1), custom_call_target="tpu_custom_call" | custom-call | tf_op jit(solution)/shard_map/pallas_call | solution.py:625
  148.3 0.0 copy-start.1
  148.3 1.7 %copy.12 = bf16[512,192]{0,1:T(8,128)(2,1)} copy(bf16[512,192]{0,1:T(8,128)(2,1)} %bitcast.7) | data formatting | bytes 393216
  149.9 0.0 copy-done.1
  149.9 0.7 copy.13
  150.6 0.0 copy-start
  150.6 2.2 %copy.14 = bf16[3,192,768]{2,1,0:T(8,128)(2,1)} copy(bf16[3,192,768]{2,1,0:T(8,128)(2,1)} %get-tuple-element.18) | data formatting | bytes 1769472
  152.8 0.0 copy-done
  152.8 0.9 copy.15
Async XLA Ops:
  148.3 1.7 %copy-start.1 = (bf16[192,512]{1,0:T(8,128)(2,1)S(1)}, bf16[192,512]{1,0:T(8,128)(2,1)}, u32[]{:S(2)}) copy-start(bf16[192,512]{1,0:T(8,128)(2,1)} %get-tuple-element.9) | copy-start | bytes 589828
  150.6 2.2 %copy-start = (bf16[3,192,768]{2,1,0:T(8,128)(2,1)S(1)}, bf16[3,192,768]{2,1,0:T(8,128)(2,1)}, u32[]{:S(2)}) copy-start(bf16[3,192,768]{2,1,0:T(8,128)(2,1)} %get-tuple-element.19) | copy-start | bytes 2654212

commit v4 on v3

--- a/solution.py
+++ b/solution.py
@@ -156,12 +156,14 @@
 
     blank(near_low, u1.at[0])
     blank(near_high, u1.at[2])
-    blank(far_low, u2.at[0])
-    blank(far_high, u2.at[2])
-    for array, low, high in ((g2, far_low, far_high), (g1, near_low, near_high)):
-        for h in (0, 1):
-            blank(high, array.at[0, h, core])
-            blank(low, array.at[2, h, core])
+    qs, qr, ts, tr = s["qs"], s["qr"], s["ts"], s["tr"]
+    blank(near_high, qr.at[0])
+    blank(near_low, qr.at[1])
+    blank(far_low, tr.at[0])
+    blank(far_high, tr.at[1])
+    for h in (0, 1):
+        blank(far_high, g2.at[0, h, core])
+        blank(far_low, g2.at[2, h, core])
 
     def lanes(m):
         return pl.ds(m * CHUNK, CHUNK)
@@ -226,7 +228,6 @@
 
     u1_own = halo(near_low, near_high, 1, u1.at[1, OWN], u1.at[2, OWN], u1.at[0, OWN], "u1h", (CHUNKS,))
     g2_core = [send(c_ref, own(g2, 1), sems("g2c"), CHUNKS, me.other_core)]
-    g2_own = halo(far_low, far_high, 4, c_ref, own(g2, 0), own(g2, 2), "g2h", (CHUNKS,))
 
     def own_cotangent(r, _):
         rows = pl.ds(pl.multiple_of(r * 16, 16), 16)
@@ -342,8 +343,8 @@
     x_chunk(2)
     halo_arrived(u1_own)
     conv_one(w1_ref, OWN, False)
-    g2_forward_own()
     x_chunk(3)
+    g2_own = halo(far_low, far_high, 4, c_ref, own(g2, 0), own(g2, 2), "g2h", (CHUNKS,))
     arrived(firsts[0])
     arrived(firsts[1])
     assemble(0, wo1)
@@ -357,7 +358,6 @@
     z1 = [send(zp.at[group_rows(h, 1 - core)], zr.at[h], sems("z1"), h, me.other_core) for h in (0, 1)]
     c_chunk(1)
     arrived(z1)
-    u2_copies = []
 
     def x1_chunk(m):
         for slot, h in ((OWN, half), (OTHER, 1 - half)):
@@ -365,17 +365,14 @@
             total = zp[group_rows(h, core), lanes(m)] + zr[h, :, lanes(m)]
             value = (before.astype(F32) + total).astype(BF16)
             x1[slot, :, lanes(m)] = value
-            u2[1, slot, :, lanes(m)] = gelu_value(value.astype(F32)).astype(BF16)
-        src = u2.at[1, :, :, lanes(m)]
-        u2_copies.extend(
-            halo(far_low, far_high, 4, src, u2.at[2, :, :, lanes(m)], u2.at[0, :, :, lanes(m)], "u2h", (m,))
-        )
+            u2[slot, :, lanes(m)] = gelu_value(value.astype(F32)).astype(BF16)
 
     for m in range(CHUNKS):
         x1_chunk(m)
     arrived(firsts[2])
     arrived(firsts[3])
     assemble(1, wo2)
+    g2_forward_own()
     g2_forward(0)
     c_chunk(2)
     g2_forward(1)
@@ -484,63 +481,67 @@
                 grad = g2[tap, 1 - half, :, :, wide].reshape(384, 256)
                 total = total + product(weight[tap, :, half_columns(1 - half)], grad)
             slope = gelu_slope(x1[slot, :, wide].astype(F32))
-            g1[1, h, core, :, wide] = (g2[1, h, core, :, wide].astype(F32) + slope * total).astype(BF16)
-        src = g1.at[1, :, core, :, wide]
+            g1[h, core, :, wide] = (g2[1, h, core, :, wide].astype(F32) + slope * total).astype(BF16)
+        src = g1.at[:, core, :, wide]
         g1_core.append(send(src, src, sems("g1c"), n, me.other_core))
 
+    weight_grad(1, lambda tap: u2[OWN], lambda tap, h: g2[tap, h])
+    for p in (0, 1):
+        reduce[1, p] = reduce_first(1, p)
     back_two(0)
     back_two(1)
-    weight_grad(1, lambda tap: u2[1, OWN], lambda tap, h: g2[tap, h])
-    for p in (0, 1):
-        reduce[1, p] = reduce_first(1, p)
     arrived(g1_core)
-    weight_grad(0, lambda tap: u1[tap, OWN], lambda tap, h: g1[1, h])
+    weight_grad(0, lambda tap: u1[tap, OWN], lambda tap, h: g1[h])
     for p in (0, 1):
         reduce[0, p] = reduce_first(0, p)
-    src = g1.at[1, :, core]
-    g1_copies = halo(near_low, near_high, 1, src, g1.at[0, :, core], g1.at[2, :, core], "g1h", (0,))
 
     yp, yr = s["yp"], s["yr"]
 
     def conv_two(n, _):
         columns = pl.ds(pl.multiple_of(half * 384 + n * 128, 128), 128)
-        total = jnp.zeros((128, ROWS), F32)
         for tap in range(3):
-            total = total + over_rows(w2_ref[tap, :, columns], u2[tap, OWN])
-            total = total + over_rows(wo2[tap, :, columns], u2[tap, OTHER])
-        yp[pl.ds(pl.multiple_of(n * 128, 128), 128)] = total
+            total = over_rows(w2_ref[tap, :, columns], u2[OWN]) + over_rows(wo2[tap, :, columns], u2[OTHER])
+            yp[tap, pl.ds(pl.multiple_of(n * 128, 128), 128)] = total
         return 0
 
+    for k, tap in enumerate((0, 2)):
+        qs[k] = product(w1_ref[tap], g1[...].reshape(768, ROWS)).astype(BF16)
+    down = send.when(near_low, qs.at[0], qr.at[0], sems("g1h"), (0, 0), me.along(-1))
+    up = send.when(near_high, qs.at[1], qr.at[1], sems("g1h"), (1, 0), me.along(1))
+    g1_copies = [(near_high, down), (near_low, up)]
+    lax.fori_loop(0, 3, conv_two, 0)
+    z2 = send(yp.at[:, pl.ds(pl.multiple_of((1 - core) * 192, 64), 192)], yr, sems("z2"), 0, me.other_core)
+    mine = pl.ds(pl.multiple_of(core * 192, 64), 192)
+
     order = [(b, p) for b in (1, 0) for p in (0, 1)]
-    halo_arrived(u2_copies)
-    lax.fori_loop(0, 3, conv_two, 0)
-    z2 = send(yp.at[pl.ds(pl.multiple_of((1 - core) * 192, 64), 192)], yr, sems("z2"), 0, me.other_core)
     for b, p in order:
         reduce[b, p] = reduce_second(b, p, reduce[b, p])
     z2.wait_recv()
-    for m in range(CHUNKS):
-        total = yp[pl.ds(pl.multiple_of(core * 192, 64), 192), lanes(m)] + yr[:, lanes(m)]
-        act_out[:, lanes(m)] = (x1[OWN, :, lanes(m)].astype(F32) + total).astype(BF16)
+    ts[0] = (yp[0, mine] + yr[0]).astype(BF16)
+    ts[1] = (yp[2, mine] + yr[2]).astype(BF16)
+    up = send.when(far_high, ts.at[0], tr.at[0], sems("u2h"), (1, 0), me.along(4))
+    down = send.when(far_low, ts.at[1], tr.at[1], sems("u2h"), (0, 0), me.along(-4))
+    u2_copies = [(far_low, up), (far_high, down)]
     for b, p in order:
         reduce[b, p] = reduce_third(b, p, reduce[b, p])
-    halo_arrived(g1_copies)
-    g1_spread = [send(g1.at[t, :, core], g1.at[t, :, core], sems("g1s"), k, me.other_core) for k, t in ((0, 0), (1, 2))]
     for b, p in order:
         reduce[b, p] = reduced(b, p, reduce[b, p])
 
-    arrived(g1_spread)
-
+    halo_arrived(g1_copies)
     for n in (0, 1):
         wide = pl.ds(n * 256, 256)
-        total = product(w1_ref[0], g1[0, :, :, :, wide].reshape(768, 256))
-        total = total + product(w1_ref[1], g1[1, :, :, :, wide].reshape(768, 256))
-        total = total + product(w1_ref[2], g1[2, :, :, :, wide].reshape(768, 256))
+        total = product(w1_ref[1], g1[:, :, :, wide].reshape(768, 256))
+        total = total + (qr[0, :, wide].astype(F32) + qr[1, :, wide].astype(F32))
         slope = gelu_slope(x_ref[:, wide].astype(F32))
-        grad_out[:, wide] = (g1[1, half, core, :, wide].astype(F32) + slope * total).astype(BF16)
-
+        grad_out[:, wide] = (g1[half, core, :, wide].astype(F32) + slope * total).astype(BF16)
     for b, p in order:
         arrived(reduce[b, p])
         reduce[b, p] = gather_second(2 * b + p, p, gh, ge, "e2")
+    halo_arrived(u2_copies)
+    for m in range(CHUNKS):
+        total = yp[1, mine, lanes(m)] + yr[1, :, lanes(m)]
+        total = total + (tr[0, :, lanes(m)].astype(F32) + tr[1, :, lanes(m)].astype(F32))
+        act_out[:, lanes(m)] = (x1[OWN, :, lanes(m)].astype(F32) + total).astype(BF16)
     for b, p in order:
         arrived(reduce[b, p])
         reduce[b, p] = gather_first(b, p, ge, gf, "e1")
@@ -575,16 +576,18 @@
     keep("xr", 192, ROWS)
     keep("x1", 2, 192, ROWS)
     keep("u1", 3, 2, 192, ROWS)
-    keep("u2", 3, 2, 192, ROWS)
+    keep("u2", 2, 192, ROWS)
     keep("g2", 3, 2, 2, 192, ROWS)
-    keep("g1", 3, 2, 2, 192, ROWS)
+    keep("g1", 2, 2, 192, ROWS)
     keep("wo1", 3, 192, 768)
     keep("wo2", 3, 192, 768)
     keep("zp", 768, ROWS, dtype=F32)
     keep("zr", 2, 192, ROWS, dtype=F32)
     keep("v", 2, 192, ROWS, dtype=F32)
-    keep("yp", 384, ROWS, dtype=F32)
-    keep("yr", 192, ROWS, dtype=F32)
+    keep("yp", 3, 384, ROWS, dtype=F32)
+    keep("yr", 3, 192, ROWS, dtype=F32)
+    for name in ("qs", "qr", "ts", "tr"):
+        keep(name, 2, 192, ROWS)
     keep("wu", 4, 16, 128)
     keep("wh", 4, 8, 16, 128)
     keep("we", 4, 32, 16, 128)
@@ -607,10 +610,10 @@
         pair(name, 4, 3)
     for name in ("u1h", "g2h", "g2s"):
         pair(name, 2, CHUNKS + 1)
-    pair("u2h", 2, CHUNKS)
+    pair("u2h", 2, 1)
     pair("g1h", 2, 1)
     pair("g2c", CHUNKS + 1)
-    for name in ("g1c", "g1s", "z1"):
+    for name in ("g1c", "z1"):
         pair(name, 2)
     pair("z2", 1)
     return table

time: 155 us -> 147 us (0.948)
  Pallas kernels: 148 us -> 138 us
    pallas_call x1, Pallas kernels: 148 us -> 138 us  [body(): pl.pallas_call(kernel, out_shape=tuple(shapes), in_specs=[vmem] * 4, out_...]
where the time goes in v4:
time: 147 us; the launch traced here: 144 us
  Pallas kernels  138 us (94%)
  local copies, waits for them, and re-layouts  5.47 us (4%)
    pallas_call x1, Pallas kernels, body(): pl.pallas_call(kernel, out_shape=tuple(shapes), in_specs=[vmem] * 4, out_...  138 us
    unnamed x8, local copies, waits for them, and re-layouts  5.47 us

profile of v4, /device:TPU:6, one launch (start us, length us, event | category | flops | bytes accessed | tf_op | source)
XLA Modules:
  0.0 144.2 jit_solution(17847008446020544801)
XLA Ops:
  0.6 138.1 %shard_map.75 = (bf16[192,512]{1,0:T(8,128)(2,1)}, bf16[192,512]{1,0:T(8,128)(2,1)}, bf16[3,192,768]{2,1,0:T(8,128)(2,1)}, bf16[3,192,768]{2,1,0:T(8,128)(2,1)}) custom-call(bf16[192,512]{1,0:T(8,128)(2,1)} %bitcast.4, bf16[192,512]{1,0:T(8,128)(2,1)} %bitcast.5, bf16[3,192,768]{2,1,0:T(8,128)(2,1)} %w1_ref.1, bf16[3,192,768]{2,1,0:T(8,128)(2,1)} %w2_ref.1), custom_call_target="tpu_custom_call" | custom-call | tf_op jit(solution)/shard_map/pallas_call | solution.py:628
  138.8 0.0 copy-start.1
  138.8 1.7 %copy.12 = bf16[512,192]{0,1:T(8,128)(2,1)} copy(bf16[512,192]{0,1:T(8,128)(2,1)} %bitcast.7) | data formatting | bytes 393216
  140.4 0.0 copy-done.1
  140.4 0.7 copy.13
  141.1 0.0 copy-start
  141.1 2.2 %copy.14 = bf16[3,192,768]{2,1,0:T(8,128)(2,1)} copy(bf16[3,192,768]{2,1,0:T(8,128)(2,1)} %get-tuple-element.18) | data formatting | bytes 1769472
  143.3 0.0 copy-done
  143.3 0.9 copy.15
Async XLA Ops:
  138.8 1.7 %copy-start.1 = (bf16[192,512]{1,0:T(8,128)(2,1)S(1)}, bf16[192,512]{1,0:T(8,128)(2,1)}, u32[]{:S(2)}) copy-start(bf16[192,512]{1,0:T(8,128)(2,1)} %get-tuple-element.9) | copy-start | bytes 589828
  141.1 2.2 %copy-start = (bf16[3,192,768]{2,1,0:T(8,128)(2,1)S(1)}, bf16[3,192,768]{2,1,0:T(8,128)(2,1)}, u32[]{:S(2)}) copy-start(bf16[3,192,768]{2,1,0:T(8,128)(2,1)} %get-tuple-element.19) | copy-start | bytes 2654212

commit v5 on v4

--- a/solution.py
+++ b/solution.py
@@ -116,8 +116,15 @@
                 pl.when(condition)(copy.wait_send)
 
 
-def kernel(x_ref, c_ref, w1_ref, w2_ref, act_out, grad_out, near_out, far_out, *scratch):
+def kernel(x_ref, c_ref, w1_hbm, w2_hbm, act_out, grad_out, near_out, far_out, *scratch):
     s = dict(zip(SCRATCH, scratch))
+    w1_ref, w2_ref = s["w1v"], s["w2v"]
+    loads = [
+        pltpu.make_async_copy(src, dst, s["load"].at[k])
+        for k, (src, dst) in enumerate(((w1_hbm, w1_ref), (w2_hbm, w2_ref)))
+    ]
+    for load in loads:
+        load.start()
     me = Place()
     half, core = me.half, me.core
     send = Sender()
@@ -178,6 +185,8 @@
     wires = 15 + sum(c.astype(jnp.int32) for c in (near_low, near_high, far_low, far_high))
     pl.semaphore_wait(barrier, wires)
 
+    for load in loads:
+        load.wait()
     weights = (w1_ref, w2_ref)
     parts = [(b, p) for b in (0, 1) for p in (0, 1)]
 
@@ -506,16 +515,16 @@
 
     for k, tap in enumerate((0, 2)):
         qs[k] = product(w1_ref[tap], g1[...].reshape(768, ROWS)).astype(BF16)
+    lax.fori_loop(0, 3, conv_two, 0)
+    z2 = send(yp.at[:, pl.ds(pl.multiple_of((1 - core) * 192, 64), 192)], yr, sems("z2"), 0, me.other_core)
+    mine = pl.ds(pl.multiple_of(core * 192, 64), 192)
+
+    order = [(b, p) for b in (1, 0) for p in (0, 1)]
+    for b, p in order:
+        reduce[b, p] = reduce_second(b, p, reduce[b, p])
     down = send.when(near_low, qs.at[0], qr.at[0], sems("g1h"), (0, 0), me.along(-1))
     up = send.when(near_high, qs.at[1], qr.at[1], sems("g1h"), (1, 0), me.along(1))
     g1_copies = [(near_high, down), (near_low, up)]
-    lax.fori_loop(0, 3, conv_two, 0)
-    z2 = send(yp.at[:, pl.ds(pl.multiple_of((1 - core) * 192, 64), 192)], yr, sems("z2"), 0, me.other_core)
-    mine = pl.ds(pl.multiple_of(core * 192, 64), 192)
-
-    order = [(b, p) for b in (1, 0) for p in (0, 1)]
-    for b, p in order:
-        reduce[b, p] = reduce_second(b, p, reduce[b, p])
     z2.wait_recv()
     ts[0] = (yp[0, mine] + yr[0]).astype(BF16)
     ts[1] = (yp[2, mine] + yr[2]).astype(BF16)
@@ -574,6 +583,9 @@
         table[name + "_r"] = pltpu.SemaphoreType.DMA(shape)
 
     keep("xr", 192, ROWS)
+    keep("w1v", 3, 192, 768)
+    keep("w2v", 3, 192, 768)
+    table["load"] = pltpu.SemaphoreType.DMA((2,))
     keep("x1", 2, 192, ROWS)
     keep("u1", 3, 2, 192, ROWS)
     keep("u2", 2, 192, ROWS)
@@ -628,7 +640,7 @@
     act, grad, near, far = pl.pallas_call(
         kernel,
         out_shape=tuple(shapes),
-        in_specs=[vmem] * 4,
+        in_specs=[vmem] * 2 + [pl.BlockSpec(memory_space=pl.ANY)] * 2,
         out_specs=(vmem,) * 4,
         scratch_shapes=list(SCRATCH.values()),
         compiler_params=pltpu.CompilerParams(

time: 147 us -> 144 us (0.980); the launches traced: 144 us -> 143 us
  no operation moved by 1% of the time
where the time goes in v5:
time: 144 us; the launch traced here: 143 us
  Pallas kernels  137 us (95%)
  local copies, waits for them, and re-layouts  5.47 us (4%)
    pallas_call x1, Pallas kernels, body(): pl.pallas_call(kernel, out_shape=tuple(shapes), in_specs=[vmem] * 2 + [pl...  137 us
    unnamed x8, local copies, waits for them, and re-layouts  5.47 us

profile of v5, /device:TPU:6, one launch (start us, length us, event | category | flops | bytes accessed | tf_op | source)
XLA Modules:
  0.0 142.9 jit_solution(6247880044728244686)
XLA Ops:
  0.6 136.8 %shard_map.75 = (bf16[192,512]{1,0:T(8,128)(2,1)}, bf16[192,512]{1,0:T(8,128)(2,1)}, bf16[3,192,768]{2,1,0:T(8,128)(2,1)}, bf16[3,192,768]{2,1,0:T(8,128)(2,1)}) custom-call(bf16[192,512]{1,0:T(8,128)(2,1)} %bitcast.4, bf16[192,512]{1,0:T(8,128)(2,1)} %bitcast.5, bf16[3,192,768]{2,1,0:T(8,128)(2,1)} %w1_hbm.1, bf16[3,192,768]{2,1,0:T(8,128)(2,1)} %w2_hbm.1), custom_call_target="tpu_custom_call" | custom-call | tf_op jit(solution)/shard_map/pallas_call | solution.py:640
  137.4 0.0 copy-start.1
  137.4 1.7 %copy.12 = bf16[512,192]{0,1:T(8,128)(2,1)} copy(bf16[512,192]{0,1:T(8,128)(2,1)} %bitcast.7) | data formatting | bytes 393216
  139.1 0.0 copy-done.1
  139.1 0.7 copy.13
  139.8 0.0 copy-start
  139.8 2.2 %copy.14 = bf16[3,192,768]{2,1,0:T(8,128)(2,1)} copy(bf16[3,192,768]{2,1,0:T(8,128)(2,1)} %get-tuple-element.18) | data formatting | bytes 1769472
  142.0 0.0 copy-done
  142.0 0.9 copy.15
Async XLA Ops:
  137.4 1.7 %copy-start.1 = (bf16[192,512]{1,0:T(8,128)(2,1)S(1)}, bf16[192,512]{1,0:T(8,128)(2,1)}, u32[]{:S(2)}) copy-start(bf16[192,512]{1,0:T(8,128)(2,1)} %get-tuple-element.9) | copy-start | bytes 589828
  139.8 2.2 %copy-start = (bf16[3,192,768]{2,1,0:T(8,128)(2,1)S(1)}, bf16[3,192,768]{2,1,0:T(8,128)(2,1)}, u32[]{:S(2)}) copy-start(bf16[3,192,768]{2,1,0:T(8,128)(2,1)} %get-tuple-element.19) | copy-start | bytes 2654212
